TPU v7x, 32 devices: a whole 2x2x4 slice. The times are simulated.
32 devices in a mesh: row: 8 (over z, x), col: 2 (over core), vec: 2 (over y).
Axes of the slice: x: 2, y: 2, z: 4, core: 2. Of those that a mesh axis runs over, the one named last changes fastest.
Arguments:
- vectors: bfloat16 [131072, 256], P(('row', 'col'), 'vec'), parts along dimension 1, may hold values from -6 to 6
- tile_blocks: bfloat16 [8, 2, 32, 256, 256], P('row', 'col'), may hold values from -0.375 to 0.375
- block_rows: int32 [8, 2, 32], P('row', 'col'), may hold values from 0 to 63, as said below
- block_cols: int32 [8, 2, 32], P('row', 'col'), may hold values from 0 to 255, as said below
- counts: int32 [8, 2], P('row', 'col'), may hold values from 1 to 32, as said below
Outputs:
- filtered: bfloat16 [131072, 256], P(('row', 'col'), 'vec'), parts along dimension 1
There are 2 independent parts, one for each index of `vec`. A program takes and returns all parts, laid end to end along the dimension named above; an argument that names none is the same for every part. Nothing has to cross between parts.
Inputs may be any that keep to these rules, and one draw needn't show every extreme that they name: The pairs (block_rows, block_cols // 32) of the 32 slots of one tile are all distinct. Within one tile, all slots whose block columns lie in the same group of 32 (same block_cols // 32) name the same block column. `counts`: some tile uses all 32 slots.
All inputs are finite; a program needn't handle non-finite values.
Results may differ from a plain program's by a relative error of at most 0.015.
Values may be sent and summed in bfloat16 or wider, within the bound.
No kernel may reach another device: no remote copies, remote signals or barrier semaphores. Data moves between devices by JAX's collectives and lax.ppermute only.
A program may use at most 64 MiB of HBM per device.

v0:
```python
import functools

import jax
import jax.numpy as jnp
from jax import lax
from jax.experimental import pallas as pl
from jax.experimental.pallas import tpu as pltpu
from jax.sharding import PartitionSpec as P

DEGREE = 3

center_value = 0.5
half_width = 2.0

VMEM = pltpu.VMEM
SMEM = pltpu.SMEM
HBM = pltpu.HBM
DMA = pltpu.SemaphoreType.DMA
LANES = 128
UNROLL = 2
HEAD = 8
STRIDE = 4
FIRST = 1
LAST = 2


def spec(space):
    return pl.BlockSpec(memory_space=space)


def params(mib):
    return pltpu.CompilerParams(vmem_limit_bytes=mib * 1024 * 1024)


def round_up(n, step):
    return (n + step - 1) // step * step


def plan_kernel(
    n_row, piece_blocks, sent_at, load_at, bare_at, place, wanted, rows_a, cols_a, used_a, meta_b, out, seen
):
    slot_count = rows_a.shape[0]
    first_row = place[1] * piece_blocks

    def scan(row_of, col_of, used, at, sent, load):
        def step(s, carry):
            at, sent, load = carry
            row = row_of(s) - first_row
            inside = (row >= 0) & (row < piece_blocks)
            mine = inside.astype(jnp.int32)
            piece = col_of(s) // piece_blocks
            kept = jnp.where(inside, row, piece_blocks)
            entry = HEAD + STRIDE * at
            out[entry] = s
            out[entry + 1] = row
            out[entry + 2] = piece
            out[entry + 3] = jnp.where(seen[kept] == 0, FIRST, 0)
            seen[kept] = entry
            out[load_at + load] = s
            before = sent
            for k in range(n_row):
                out[sent_at + STRIDE * sent] = load
                out[sent_at + STRIDE * sent + 1] = k
                out[sent_at + STRIDE * sent + 2] = piece
                sent = sent + jnp.where(wanted[k, 0] == row, mine, 0)
            return at + mine, sent, load + (sent > before).astype(jnp.int32)

        at, sent, load = lax.fori_loop(0, used, step, (at, sent, load))
        for _ in range(UNROLL):
            for base, end, spare in ((HEAD, at, piece_blocks), (sent_at, sent, n_row)):
                entry = base + STRIDE * end
                out[entry] = 0
                out[entry + 1] = spare
                out[entry + 2] = 0
                out[entry + 3] = 0
            at = at + jnp.where(at % UNROLL == 0, 0, 1)
            sent = sent + jnp.where(sent % UNROLL == 0, 0, 1)
        return at, sent, load

    for b in range(piece_blocks + 1):
        seen[b] = 0
    zero = jnp.int32(0)
    at, sent, load = scan(
        lambda s: rows_a[s], lambda s: cols_a[s], used_a[0], zero, zero, zero
    )
    out[0] = at
    out[2] = sent
    out[4] = load
    at, sent, load = scan(
        lambda s: meta_b[s],
        lambda s: meta_b[slot_count + s],
        meta_b[2 * slot_count],
        at,
        sent,
        load,
    )
    out[1] = at
    out[3] = sent
    out[5] = load

    def close(b, bare):
        entry = seen[b]
        out[bare_at + bare] = b

        @pl.when(entry > 0)
        def _():
            out[entry + 3] = out[entry + 3] + LAST

        return bare + jnp.where(entry == 0, 1, 0)

    out[6] = lax.fori_loop(0, piece_blocks, close, zero)


def pick_kernel(n_row, block_size, wanted, vectors, out, held, in_sems, out_sems):
    def fetch(k):
        at = pl.multiple_of(wanted[k, 0] * block_size, block_size)
        return pltpu.make_async_copy(vectors.at[pl.ds(at, block_size)], held.at[k], in_sems.at[k])

    def put(k):
        return pltpu.make_async_copy(held.at[k], out.at[k], out_sems.at[k])

    for k in range(n_row):
        fetch(k).start()
    for k in range(n_row):
        fetch(k).wait()
        put(k).start()
    for k in range(n_row):
        put(k).wait()


def load_kernel(base, stride, ends, plan, tile_a, tile_b, blocks, sems):
    mid, end = plan[ends], plan[ends + 1]

    def copy(tile, i):
        slot = plan[base + stride * i]
        return pltpu.make_async_copy(tile.at[slot], blocks.at[i], sems.at[i])

    @pl.loop(0, mid)
    def _(i):
        copy(tile_a, i).start()

    @pl.loop(mid, end)
    def _(i):
        copy(tile_b, i).start()

    @pl.loop(0, end)
    def _(i):
        copy(tile_a, i).wait()


def load_both_kernel(base, stride, ends, plan, tile_a, tile_b, array, blocks, held, sems, held_sem):
    copy = pltpu.make_async_copy(array, held, held_sem)
    copy.start()
    load_kernel(base, stride, ends, plan, tile_a, tile_b, blocks, sems)
    copy.wait()


def each_product(plan, base, ends, blocks, pieces, use, then=None):
    mid, end = plan[ends], plan[ends + 1]

    def run(piece_ref, begin, end):
        @pl.loop(begin // UNROLL, end // UNROLL)
        def _(j):
            for u in range(UNROLL):
                i = UNROLL * j + u
                entry = base + STRIDE * i
                block = blocks[i if base == HEAD else plan[entry]]
                use(
                    entry,
                    jnp.dot(block, piece_ref[plan[entry + 2]], preferred_element_type=jnp.float32),
                )
            if then is not None:
                for u in range(UNROLL):
                    then(base + STRIDE * (UNROLL * j + u))

    run(pieces[0], 0, mid)
    run(pieces[1], mid, end)


def add_products(plan, base, ends, blocks, pieces, total):
    def use(entry, value):
        total[plan[entry + 1]] += value

    each_product(plan, base, ends, blocks, pieces, use)


def sent_kernel(first, sent_at, plan, blocks, pieces, others, picked, *rest):
    if first:
        out, total, held, held_sem = rest
    else:
        current, out, total, held, held_sem, ready, out_sems = rest
    n_row = out.shape[0]
    copy = pltpu.make_async_copy(picked, held, held_sem)
    copy.start()
    for k in range(n_row):
        if first:
            total[k] = jnp.zeros(total.shape[1:], jnp.float32)
        else:
            total[k] = -center_value * current[k].astype(jnp.float32)
    add_products(plan, sent_at, 2, blocks, (pieces, others), total)
    copy.wait()
    if first:
        for k in range(n_row):
            value = total[k] - center_value * held[k].astype(jnp.float32)
            out[k] = (value / half_width).astype(jnp.bfloat16)
        return

    def put(k):
        return pltpu.make_async_copy(ready.at[k], out.at[k], out_sems.at[k])

    for k in range(n_row):
        ready[k] = (total[k] - held[k].astype(jnp.float32)).astype(jnp.bfloat16)
        put(k).start()
    for k in range(n_row):
        put(k).wait()


def early_kernel(plan, blocks, p1, p2, o1, o2, vectors, base, vec, total, own, sems, row_sems):
    width = vectors.shape[1]
    piece_blocks, block_size, _ = base.shape
    copies = [
        pltpu.make_async_copy(
            source, vec.at[side, :, :, pl.ds(step * width, width)], sems.at[2 * side + step]
        )
        for side, step, source in ((0, 0, p1), (0, 1, p2), (1, 0, o1), (1, 1, o2))
    ]
    copies.append(pltpu.make_async_copy(vectors, own, sems.at[4]))
    for copy in copies:
        copy.start()
    copies[-1].wait()

    def rows(b):
        return pl.ds(pl.multiple_of(b * block_size, block_size), block_size)

    def put(b):
        return pltpu.make_async_copy(own.at[rows(b)], base.at[b], row_sems.at[b])

    @pl.loop(0, piece_blocks)
    def _(b):
        value = own[rows(b), :].astype(jnp.float32)
        total[b, :, :width] = -center_value * value
        total[b, :, width:] = -value

    for copy in copies[:-1]:
        copy.wait()
    add_products(plan, HEAD, 0, blocks, (vec.at[0], vec.at[1]), total)

    @pl.loop(0, piece_blocks)
    def _(b):
        first = (total[b, :, :width] / half_width).astype(jnp.bfloat16).astype(jnp.float32)
        second = total[b, :, width:] - center_value * first
        second = second.astype(jnp.bfloat16).astype(jnp.float32)
        own[rows(b), :] = (-center_value * second - first).astype(jnp.bfloat16)
        put(b).start()

    @pl.loop(0, piece_blocks)
    def _(b):
        put(b).wait()


def last_kernel(bare_at, plan, blocks, pieces, others, base, out, total, own, row_sems):
    piece_blocks = base.shape[0]

    def put(source, b):
        return pltpu.make_async_copy(source.at[b], out.at[b], row_sems.at[b])

    @pl.loop(0, plan[6])
    def _(i):
        b = plan[bare_at + i]
        put(base, b).start()

    def use(entry, value):
        row = plan[entry + 1]
        marks = plan[entry + 3]
        start = base[jnp.minimum(row, piece_blocks - 1)].astype(jnp.float32)
        value = jnp.where(lax.rem(marks, LAST) == FIRST, start, total[row]) + value
        total[row] = value
        own[row] = value.astype(jnp.bfloat16)

    def then(entry):
        @pl.when(plan[entry + 3] >= LAST)
        def _():
            put(own, plan[entry + 1]).start()

    each_product(plan, HEAD, 0, blocks, (pieces, others), use, then)

    @pl.loop(0, piece_blocks)
    def _(b):
        put(own, b).wait()


def after(value, *others):
    return lax.optimization_barrier((value, *others))[0]


def call(kernel, out, args, spaces, scratch, mib, name, estimate=None):
    args = [
        pltpu.with_memory_space_constraint(arg, space) if space in (VMEM, HBM) or tied else arg
        for arg, (space, tied) in zip(args, spaces)
    ]
    return pl.pallas_call(
        kernel,
        out_shape=[space(shape, dtype) for shape, dtype, space in out],
        in_specs=[spec(space) for space, _ in spaces],
        out_specs=[spec(space) for _, _, space in out],
        scratch_shapes=scratch,
        compiler_params=params(mib),
        cost_estimate=estimate,
        name=name,
    )(*args)


HERE = (VMEM, True)
FAR = (HBM, True)
LIST = (SMEM, True)
SCALARS = (SMEM, False)
ANYWHERE = (pl.ANY, False)


def on_pair(vectors, tile_blocks, block_rows, block_cols, counts):
    n_row = lax.axis_size("row")
    tile = tile_blocks[0, 0]
    slot_rows = block_rows[0, 0]
    slot_cols = block_cols[0, 0]
    used = counts[0]
    slot_count, block_size, _ = tile.shape
    width = vectors.shape[1]
    piece_blocks = vectors.shape[0] // block_size
    place = jnp.stack([lax.axis_index("row"), lax.axis_index("col")]).astype(jnp.int32)

    across = functools.partial(lax.ppermute, axis_name="col", perm=[(0, 1), (1, 0)])

    needed = jnp.max(
        jnp.where(
            slot_cols[None, :] // piece_blocks == jnp.arange(n_row)[:, None],
            slot_cols[None, :] % piece_blocks,
            0,
        ),
        axis=1,
        keepdims=True,
    )
    exchange = functools.partial(
        lax.all_to_all, axis_name="row", split_axis=0, concat_axis=0, tiled=True
    )
    wanted = exchange(jnp.broadcast_to(needed, (n_row, LANES)))
    sent_shape = (n_row, block_size, width)
    (sent,) = call(
        functools.partial(pick_kernel, n_row, block_size),
        [(sent_shape, jnp.bfloat16, HBM)],
        (wanted, vectors),
        (SCALARS, FAR),
        [VMEM(sent_shape, jnp.bfloat16), DMA((n_row,)), DMA((n_row,))],
        2,
        "pick",
    )
    tile_other = across(after(tile, sent))
    meta = across(after(jnp.concatenate([slot_rows, slot_cols, used]), sent))

    capacity = 2 * round_up(slot_count, UNROLL)
    sent_at = HEAD + STRIDE * (capacity + 1)
    load_at = sent_at + STRIDE * (2 * n_row * n_row + 2 * UNROLL + 1)
    bare_at = load_at + 2 * slot_count + 1
    plan_size = bare_at + piece_blocks
    (plan,) = call(
        functools.partial(plan_kernel, n_row, piece_blocks, sent_at, load_at, bare_at),
        [((plan_size,), jnp.int32, SMEM)],
        (place, wanted, slot_rows, slot_cols, used, meta),
        (SCALARS,) * 6,
        [SMEM((piece_blocks + 1,), jnp.int32)],
        2,
        "plan",
    )
    def load(base, stride, ends, cue, *array):
        kernel = load_both_kernel if array else load_kernel
        return call(
            functools.partial(kernel, base, stride, ends),
            [((capacity, block_size, block_size), jnp.bfloat16, VMEM)]
            + [(held.shape, held.dtype, VMEM) for held in array],
            (after(plan, cue), tile, tile_other, *array),
            (LIST, FAR, ANYWHERE) + (FAR,) * len(array),
            [DMA((capacity,))] + [DMA] * len(array),
            2,
            "load",
        )

    def cost(products, rows):
        size = block_size * width
        return pl.CostEstimate(
            flops=2 * products * block_size * size,
            bytes_accessed=2 * (products * block_size * block_size + 3 * rows * size),
            transcendentals=0,
        )

    def sent_blocks(blocks, *args):
        first = len(args) == 3
        held = [VMEM(sent_shape, jnp.bfloat16), DMA]
        staged = [] if first else [VMEM(sent_shape, jnp.bfloat16), DMA((n_row,))]
        return call(
            functools.partial(sent_kernel, first, sent_at),
            [(sent_shape, jnp.bfloat16, VMEM if first else HBM)],
            (plan, blocks, *args),
            (LIST, HERE, HERE, HERE, FAR) + (HERE,) * (len(args) - 3),
            [VMEM((n_row + 1, block_size, width), jnp.float32)] + held + staged,
            4,
            "sent",
            cost(n_row, n_row),
        )[0]

    base_shape = (piece_blocks, block_size, width)

    def early(blocks, *pieces):
        return call(
            early_kernel,
            [(base_shape, jnp.bfloat16, HBM)],
            (plan, blocks, *pieces, vectors),
            (LIST,) + (HERE,) * 5 + (FAR,),
            [
                VMEM((2, n_row, block_size, 2 * width), jnp.bfloat16),
                VMEM((piece_blocks + 1, block_size, 2 * width), jnp.float32),
                VMEM(vectors.shape, jnp.bfloat16),
                DMA((5,)),
                DMA((piece_blocks,)),
            ],
            18,
            "early",
            cost(2 * slot_count, 2 * piece_blocks),
        )[0]

    def last(blocks, *args):
        rows = (piece_blocks + 1, block_size, width)
        (out,) = call(
            functools.partial(last_kernel, bare_at),
            [(base_shape, jnp.bfloat16, HBM)],
            (plan, blocks, *args),
            (LIST,) + (HERE,) * 4,
            [VMEM(rows, jnp.float32), VMEM(rows, jnp.bfloat16), DMA((piece_blocks,))],
            8,
            "last",
            cost(slot_count, piece_blocks),
        )
        return out.reshape(vectors.shape)

    p1 = after(exchange(sent), plan)
    o1 = across(p1)
    (blocks,) = load(load_at, 1, 4, p1)
    first_sent = sent_blocks(blocks, p1, o1, sent)
    p2 = exchange(first_sent)
    o2 = across(p2)
    second_sent = sent_blocks(blocks, p2, o2, sent, first_sent)
    (blocks,) = load(HEAD, STRIDE, 0, second_sent)
    base = early(blocks, p1, p2, o1, o2)
    p3 = after(exchange(second_sent), base)
    o3 = across(p3)
    blocks, base = load(HEAD, STRIDE, 0, p3, base)
    return last(blocks, p3, o3, base)


def on_any(vectors, tile_blocks, block_rows, block_cols, counts):
    n_row = lax.axis_size("row")
    n_col = lax.axis_size("col")
    tile_data = tile_blocks[0, 0]
    slot_rows = block_rows[0, 0]
    slot_cols = block_cols[0, 0]
    used = counts[0, 0]
    block_size = tile_data.shape[-1]
    width = vectors.shape[1]
    piece_blocks = vectors.shape[0] // block_size
    row_blocks = piece_blocks * n_col
    slot_count = tile_data.shape[0]
    live = (jnp.arange(slot_count) < used).astype(jnp.float32)
    onehot = (slot_rows[None, :] == jnp.arange(row_blocks)[:, None]).astype(jnp.float32) * live[
        None, :
    ]
    source_piece = slot_cols // piece_blocks
    offset = slot_cols % piece_blocks
    needed = jnp.max(
        jnp.where(source_piece[None, :] == jnp.arange(n_row)[:, None], offset[None, :], 0), axis=1
    )
    wanted = lax.all_to_all(
        needed.reshape(n_row, 1), "row", split_axis=0, concat_axis=0, tiled=True
    ).reshape(n_row)

    def apply_tiles(current):
        own_blocks = current.reshape(piece_blocks, block_size, width)
        outgoing = jnp.take(own_blocks, wanted, axis=0)
        received = lax.all_to_all(outgoing, "row", split_axis=0, concat_axis=0, tiled=True)
        vec_blocks = jnp.take(received, source_piece, axis=0)
        products = jnp.einsum(
            "sij,sjk->sik", tile_data, vec_blocks, preferred_element_type=jnp.float32
        )
        term = jnp.einsum("ls,sik->lik", onehot, products, precision=lax.Precision.HIGHEST)
        term = term.reshape(row_blocks * block_size, width)
        return lax.psum_scatter(
            term.astype(jnp.bfloat16), "col", scatter_dimension=0, tiled=True
        ).astype(jnp.float32)

    previous = vectors
    applied = apply_tiles(vectors)
    current = ((applied - center_value * previous.astype(jnp.float32)) / half_width).astype(
        jnp.bfloat16
    )
    for repeat in range(DEGREE - 1):
        applied = apply_tiles(current)
        following = (
            2.0 * (applied - center_value * current.astype(jnp.float32)) / half_width
            - previous.astype(jnp.float32)
        ).astype(jnp.bfloat16)
        previous, current = (current, following)
    return current


def solution(mesh):
    n_row, n_col = mesh.shape["row"], mesh.shape["col"]
    paired = n_col == 2 and n_row & (n_row - 1) == 0
    return jax.shard_map(
        on_pair if paired else on_any,
        mesh=mesh,
        in_specs=(
            P(("row", "col"), "vec"),
            P("row", "col", None, None, None),
            P("row", "col", None),
            P("row", "col", None),
            P("row", "col"),
        ),
        out_specs=P(("row", "col"), "vec"),
        check_vma=False,
    )
```

profile of v0, /device:TPU:0, one launch (start us, length us, event | category | flops | bytes accessed | tf_op | source)
XLA Modules:
  0.0 87.4 jit_solution(15968264847790153267)
XLA Ops:
  0.0 0.7 and_select_fusion.1
  0.7 0.1 select_reduce_fusion
  0.9 13.5 %all_to_all.23 = s32[8,1,128]{2,1,0:T(1,128)S(1)} all-to-all(s32[8,1,128]{2,1,0:T(1,128)S(1)} %broadcast_in_dim.21), channel_id=1, replica_groups=mesh['row'=8,'col'=2,'vec'=2] {'row'}, dimensions={0} | all-to-all | bytes 8192 | tf_op jit(solution)/shard_map/all_to_all | solution.py:345
  14.4 2.4 %pick.1.picked = bf16[8,256,128]{2,1,0:T(8,128)(2,1)} custom-call(s32[8,128]{1,0:T(8,128)S(1)} %bitcast.16, bf16[8192,128]{1,0:T(8,128)(2,1)} %vectors.3), custom_call_target="tpu_custom_call" | custom-call | tf_op jit(solution)/shard_map/pick/pallas_call | solution.py:301
  16.9 3.5 %all-to-all-start.1 = ((bf16[8,256,128]{2,1,0:T(8,128)(2,1)}), bf16[8,256,128]{2,1,0:T(8,128)(2,1)S(1)}, u32[]{:S(2)}, u32[]{:S(2)}) async-start(bf16[8,256,128]{2,1,0:T(8,128)(2,1)} %pick.1.picked), calls=%async_computation.1 | async-start | bytes 1048576 | tf_op jit(solution)/shard_map/all_to_all | solution.py:443
  21.1 0.8 pad_add_fusion.1
  21.8 0.5 collective-permute-start
  22.4 1.6 %collective-permute-done.meta_b = s32[65]{0:T(128)S(1)} collective-permute-done((s32[65]{0:T(128)S(1)}, s32[65]{0:T(128)S(1)}, u32[]{:S(2)}, u32[]{:S(2)}) %collective-permute-start) | collective-permute-done | bytes 292 | tf_op jit(solution)/shard_map/ppermute | solution.py:357
  24.0 0.7 copy-done
  24.7 0.7 copy-done.1
  25.3 3.0 %plan.1 = s32[897]{0:T(1024)S(4)} custom-call(s32[2]{0:T(128)S(1)} %pad_add_fusion.place, s32[8,128]{1,0:T(8,128)S(1)} %bitcast.17, s32[32]{0:T(128)S(1)} %bitcast.21, s32[32]{0:T(128)S(1)} %bitcast.19, s32[1]{0:T(128)} %bitcast.15.used_a, s32[65]{0:T(128)S(1)} %collective-permute-done.meta_b), custom_call_target="tpu_custom_call" | custom-call | tf_op jit(solution)/shard_map/plan/pallas_call | solution.py:301
  28.4 7.4 %all-to-all-done.1.pieces.p1 = bf16[8,256,128]{2,1,0:T(8,128)(2,1)S(1)} async-done(((bf16[8,256,128]{2,1,0:T(8,128)(2,1)}), bf16[8,256,128]{2,1,0:T(8,128)(2,1)S(1)}, u32[]{:S(2)}, u32[]{:S(2)}) %all-to-all-start.1) | async-done | bytes 524320 | tf_op jit(solution)/shard_map/all_to_all | solution.py:443
  35.8 1.7 %load.3.blocks = bf16[64,256,256]{2,1,0:T(8,128)(2,1)S(1)} custom-call(s32[897]{0:T(1024)S(4)} %plan.1, bf16[32,256,256]{2,1,0:T(8,128)(2,1)} %bitcast.23, bf16[32,256,256]{2,1,0:T(8,128)(2,1)} %collective-permute-done.1.tile_b), custom_call_target="tpu_custom_call" | custom-call | tf_op jit(solution)/shard_map/load/pallas_call | solution.py:301
  37.5 0.2 collective-permute-done.2.others.o1
  37.7 1.2 %sent.2.rest_0_ = bf16[8,256,128]{2,1,0:T(8,128)(2,1)S(1)} custom-call(s32[897]{0:T(1024)S(4)} %plan.1, bf16[64,256,256]{2,1,0:T(8,128)(2,1)S(1)} %load.3.blocks, bf16[8,256,128]{2,1,0:T(8,128)(2,1)S(1)} %all-to-all-done.1.pieces.p1, bf16[8,256,128]{2,1,0:T(8,128)(2,1)S(1)} %collective-permute-done.2.others.o1, bf16[8,256,128]{2,1,0:T(8,128)(2,1)} %pick.1.picked), custom_call_target="tpu_custom_call" | custom-call | flops 134217728 | bytes 2621440 | tf_op jit(solution)/shard_map/sent/pallas_call | solution.py:301
  38.9 18.5 %all_to_all.24.pieces.p2 = bf16[8,256,128]{2,1,0:T(8,128)(2,1)S(1)} all-to-all(bf16[8,256,128]{2,1,0:T(8,128)(2,1)S(1)} %sent.2.rest_0_), channel_id=1, replica_groups=mesh['row'=8,'col'=2,'vec'=2] {'row'}, dimensions={0} | all-to-all | bytes 1048576 | tf_op jit(solution)/shard_map/all_to_all | solution.py:447
  57.5 1.9 %collective-permute-done.3.others.o2 = bf16[8,256,128]{2,1,0:T(8,128)(2,1)S(1)} collective-permute-done((bf16[8,256,128]{2,1,0:T(8,128)(2,1)S(1)}, bf16[8,256,128]{2,1,0:T(8,128)(2,1)S(1)}, u32[]{:S(2)}, u32[]{:S(2)}) %collective-permute-start.3) | collective-permute-done | bytes 524320 | tf_op jit(solution)/shard_map/ppermute | solution.py:448
  59.4 1.9 %sent.3 = bf16[8,256,128]{2,1,0:T(8,128)(2,1)} custom-call(s32[897]{0:T(1024)S(4)} %plan.1, bf16[64,256,256]{2,1,0:T(8,128)(2,1)S(1)} %load.3.blocks, bf16[8,256,128]{2,1,0:T(8,128)(2,1)S(1)} %all_to_all.24.pieces.p2, bf16[8,256,128]{2,1,0:T(8,128)(2,1)S(1)} %collective-permute-done.3.others.o2, bf16[8,256,128]{2,1,0:T(8,128)(2,1)} %pick.1.picked, ...), custom_call_target="tpu_custom_call" | custom-call | flops 134217728 | bytes 2621440 | tf_op jit(solution)/shard_map/sent/pallas_call | solution.py:301
  61.3 3.8 %all-to-all-start.3 = ((bf16[8,256,128]{2,1,0:T(8,128)(2,1)}), bf16[8,256,128]{2,1,0:T(8,128)(2,1)S(1)}, u32[]{:S(2)}, u32[]{:S(2)}) async-start(bf16[8,256,128]{2,1,0:T(8,128)(2,1)} %sent.3), calls=%async_computation.3 | async-start | bytes 1048576 | tf_op jit(solution)/shard_map/all_to_all | solution.py:452
  65.1 2.7 %load.4.blocks = bf16[64,256,256]{2,1,0:T(8,128)(2,1)S(1)} custom-call(s32[897]{0:T(1024)S(4)} %plan.1, bf16[32,256,256]{2,1,0:T(8,128)(2,1)} %bitcast.24, bf16[32,256,256]{2,1,0:T(8,128)(2,1)} %collective-permute-done.1.tile_b), custom_call_target="tpu_custom_call" | custom-call | tf_op jit(solution)/shard_map/load/pallas_call | solution.py:301
  67.8 8.6 %early.1.array = bf16[32,256,128]{2,1,0:T(8,128)(2,1)} custom-call(s32[897]{0:T(1024)S(4)} %plan.1, bf16[64,256,256]{2,1,0:T(8,128)(2,1)S(1)} %load.4.blocks, bf16[8,256,128]{2,1,0:T(8,128)(2,1)S(1)} %all-to-all-done.1.pieces.p1, bf16[8,256,128]{2,1,0:T(8,128)(2,1)S(1)} %all_to_all.24.pieces.p2, bf16[8,256,128]{2,1,0:T(8,128)(2,1)S(1)} %collective-permute-done.2.others.o1, ...), custom_call_target="tpu_custom_call" | custom-call | flops 1073741824 | bytes 20971520 | tf_op jit(solution)/shard_map/early/pallas_call | solution.py:301
  76.5 3.3 %all-to-all-done.3.pieces = bf16[8,256,128]{2,1,0:T(8,128)(2,1)S(1)} async-done(((bf16[8,256,128]{2,1,0:T(8,128)(2,1)}), bf16[8,256,128]{2,1,0:T(8,128)(2,1)S(1)}, u32[]{:S(2)}, u32[]{:S(2)}) %all-to-all-start.3) | async-done | bytes 524320 | tf_op jit(solution)/shard_map/all_to_all | solution.py:452
  79.8 3.2 %load.5 = (bf16[64,256,256]{2,1,0:T(8,128)(2,1)S(1)}, bf16[32,256,128]{2,1,0:T(8,128)(2,1)S(1)}) custom-call(s32[897]{0:T(1024)S(4)} %plan.1, bf16[32,256,256]{2,1,0:T(8,128)(2,1)} %bitcast.25, bf16[32,256,256]{2,1,0:T(8,128)(2,1)} %collective-permute-done.1.tile_b, bf16[32,256,128]{2,1,0:T(8,128)(2,1)} %early.1.array), custom_call_target="tpu_custom_call" | custom-call | tf_op jit(solution)/shard_map/load/pallas_call | solution.py:301
  83.0 4.4 %last.1 = bf16[32,256,128]{2,1,0:T(8,128)(2,1)} custom-call(s32[897]{0:T(1024)S(4)} %plan.1, bf16[64,256,256]{2,1,0:T(8,128)(2,1)S(1)} %get-tuple-element.21.blocks, bf16[8,256,128]{2,1,0:T(8,128)(2,1)S(1)} %all-to-all-done.3.pieces, bf16[8,256,128]{2,1,0:T(8,128)(2,1)S(1)} %collective-permute-done.4.others, bf16[32,256,128]{2,1,0:T(8,128)(2,1)S(1)} %get-tuple-element.22.base), custom_call_target="tpu_custom_call" | custom-call | flops 536870912 | bytes 10485760 | tf_op jit(solution)/shard_map/last/pallas_call | solution.py:301
  (10 shorter events, 0.2 us)
Async XLA Ops:
  16.8 19.0 %collective-permute-start.1 = (bf16[32,256,256]{2,1,0:T(8,128)(2,1)}, bf16[32,256,256]{2,1,0:T(8,128)(2,1)}, u32[]{:S(2)}, u32[]{:S(2)}) collective-permute-start(bf16[32,256,256]{2,1,0:T(8,128)(2,1)} %bitcast.22), channel_id=1, source_target_pairs={{0,2},{2,0},{1,3},{3,1},{4,6},{6,4},{5,7},{7,5},{8,10},{10,8},{9,1... | collective-permute-start | bytes 12582920 | tf_op jit(solution)/shard_map/ppermute | solution.py:356
  16.9 18.9 %all-to-all-start.1 = ((bf16[8,256,128]{2,1,0:T(8,128)(2,1)}), bf16[8,256,128]{2,1,0:T(8,128)(2,1)S(1)}, u32[]{:S(2)}, u32[]{:S(2)}) async-start(bf16[8,256,128]{2,1,0:T(8,128)(2,1)} %pick.1.picked), calls=%async_computation.1 | async-start | bytes 1048576 | tf_op jit(solution)/shard_map/all_to_all | solution.py:443
  21.8 2.2 %collective-permute-start = (s32[65]{0:T(128)S(1)}, s32[65]{0:T(128)S(1)}, u32[]{:S(2)}, u32[]{:S(2)}) collective-permute-start(s32[65]{0:T(128)S(1)} %pad_add_fusion.1), channel_id=1, source_target_pairs={{0,2},{2,0},{1,3},{3,1},{4,6},{6,4},{5,7},{7,5},{8,10},{10,8},{9,1... | collective-permute-start | bytes 788 | tf_op jit(solution)/shard_map/ppermute | solution.py:357
  24.0 0.7 copy-start
  24.7 0.7 copy-start.1
  35.8 1.9 %collective-permute-start.2 = (bf16[8,256,128]{2,1,0:T(8,128)(2,1)S(1)}, bf16[8,256,128]{2,1,0:T(8,128)(2,1)S(1)}, u32[]{:S(2)}, u32[]{:S(2)}) collective-permute-start(bf16[8,256,128]{2,1,0:T(8,128)(2,1)S(1)} %all-to-all-done.1.pieces.p1), channel_id=1, source_target_pairs={{0,2},{2,0},{1,3},{3,1},{4,6},{6,4},{5,7},{7,5},{8,10},{10,8},{9,1... | collective-permute-start | bytes 1572872 | tf_op jit(solution)/shard_map/ppermute | solution.py:444
  57.4 1.9 %collective-permute-start.3 = (bf16[8,256,128]{2,1,0:T(8,128)(2,1)S(1)}, bf16[8,256,128]{2,1,0:T(8,128)(2,1)S(1)}, u32[]{:S(2)}, u32[]{:S(2)}) collective-permute-start(bf16[8,256,128]{2,1,0:T(8,128)(2,1)S(1)} %all_to_all.24.pieces.p2), channel_id=1, source_target_pairs={{0,2},{2,0},{1,3},{3,1},{4,6},{6,4},{5,7},{7,5},{8,10},{10,8},{9,1... | collective-permute-start | bytes 1572872 | tf_op jit(solution)/shard_map/ppermute | solution.py:448
  61.3 18.5 %all-to-all-start.3 = ((bf16[8,256,128]{2,1,0:T(8,128)(2,1)}), bf16[8,256,128]{2,1,0:T(8,128)(2,1)S(1)}, u32[]{:S(2)}, u32[]{:S(2)}) async-start(bf16[8,256,128]{2,1,0:T(8,128)(2,1)} %sent.3), calls=%async_computation.3 | async-start | bytes 1048576 | tf_op jit(solution)/shard_map/all_to_all | solution.py:452
  79.8 3.2 %collective-permute-start.4 = (bf16[8,256,128]{2,1,0:T(8,128)(2,1)S(1)}, bf16[8,256,128]{2,1,0:T(8,128)(2,1)S(1)}, u32[]{:S(2)}, u32[]{:S(2)}) collective-permute-start(bf16[8,256,128]{2,1,0:T(8,128)(2,1)S(1)} %all-to-all-done.3.pieces), channel_id=1, source_target_pairs={{0,2},{2,0},{1,3},{3,1},{4,6},{6,4},{5,7},{7,5},{8,10},{10,8},{9,1... | collective-permute-start | bytes 1572872 | tf_op jit(solution)/shard_map/ppermute | solution.py:453
where the time goes:
time: 87.3 us; the launch traced here: 87.4 us
  blocking collectives  32 us (37%)
  Pallas kernels  29.2 us (33%)
  waiting for transfers between devices  14.5 us (17%)
  starting transfers between devices  7.91 us (9%)
  other arithmetic  1.61 us (2%)
  local copies, waits for them, and re-layouts  1.38 us (2%)
    pallas_call x9, Pallas kernels, call(): pl.pallas_call(kernel, out_shape=[space(shape, dtype) for shape, dtype, s...  29.2 us
    all_to_all x1, blocking collectives, on_pair(): p2 = exchange(first_sent)  18.5 us
    all_to_all x1, blocking collectives, on_pair(): wanted = exchange(jnp.broadcast_to(needed, (n_row, LANES)))  13.5 us
    all_to_all x1, waiting for transfers between devices, on_pair(): p1 = after(exchange(sent), plan)  7.43 us
    all_to_all x1, starting transfers between devices, on_pair(): p3 = after(exchange(second_sent), base)  3.83 us
    all_to_all x1, starting transfers between devices, on_pair(): p1 = after(exchange(sent), plan)  3.51 us
    all_to_all x1, waiting for transfers between devices, on_pair(): p3 = after(exchange(second_sent), base)  3.34 us
    ppermute x1, waiting for transfers between devices, on_pair(): o2 = across(p2)  1.91 us
  transfers between devices with their start and end apart: 7, of which 5 were waited for; matrix products, arithmetic and copies ran while one was open for 1% of the time, Pallas kernels for 22%

commit v1 on v0

--- a/solution.py
+++ b/solution.py
@@ -17,7 +17,8 @@
 HBM = pltpu.HBM
 DMA = pltpu.SemaphoreType.DMA
 LANES = 128
-UNROLL = 2
+FEW = 2
+MANY = 4
 HEAD = 8
 STRIDE = 4
 FIRST = 1
@@ -66,15 +67,15 @@
             return at + mine, sent, load + (sent > before).astype(jnp.int32)
 
         at, sent, load = lax.fori_loop(0, used, step, (at, sent, load))
-        for _ in range(UNROLL):
+        for _ in range(MANY):
             for base, end, spare in ((HEAD, at, piece_blocks), (sent_at, sent, n_row)):
                 entry = base + STRIDE * end
                 out[entry] = 0
                 out[entry + 1] = spare
                 out[entry + 2] = 0
                 out[entry + 3] = 0
-            at = at + jnp.where(at % UNROLL == 0, 0, 1)
-            sent = sent + jnp.where(sent % UNROLL == 0, 0, 1)
+            at = at + jnp.where(at % MANY == 0, 0, 1)
+            sent = sent + jnp.where(sent % FEW == 0, 0, 1)
         return at, sent, load
 
     for b in range(piece_blocks + 1):
@@ -157,12 +158,13 @@
 
 def each_product(plan, base, ends, blocks, pieces, use, then=None):
     mid, end = plan[ends], plan[ends + 1]
+    unroll = MANY if base == HEAD else FEW
 
     def run(piece_ref, begin, end):
-        @pl.loop(begin // UNROLL, end // UNROLL)
+        @pl.loop(begin // unroll, end // unroll)
         def _(j):
-            for u in range(UNROLL):
-                i = UNROLL * j + u
+            for u in range(unroll):
+                i = unroll * j + u
                 entry = base + STRIDE * i
                 block = blocks[i if base == HEAD else plan[entry]]
                 use(
@@ -170,8 +172,8 @@
                     jnp.dot(block, piece_ref[plan[entry + 2]], preferred_element_type=jnp.float32),
                 )
             if then is not None:
-                for u in range(UNROLL):
-                    then(base + STRIDE * (UNROLL * j + u))
+                for u in range(unroll):
+                    then(base + STRIDE * (unroll * j + u))
 
     run(pieces[0], 0, mid)
     run(pieces[1], mid, end)
@@ -356,9 +358,9 @@
     tile_other = across(after(tile, sent))
     meta = across(after(jnp.concatenate([slot_rows, slot_cols, used]), sent))
 
-    capacity = 2 * round_up(slot_count, UNROLL)
+    capacity = 2 * round_up(slot_count, MANY)
     sent_at = HEAD + STRIDE * (capacity + 1)
-    load_at = sent_at + STRIDE * (2 * n_row * n_row + 2 * UNROLL + 1)
+    load_at = sent_at + STRIDE * (2 * n_row * n_row + 2 * FEW + 1)
     bare_at = load_at + 2 * slot_count + 1
     plan_size = bare_at + piece_blocks
     (plan,) = call(

time: 87.3 us -> 87.1 us (level); the launches traced: 87.4 us -> 85.7 us
  Pallas kernels: 29.2 us -> 24.7 us
  waiting for transfers between devices: 14.5 us -> 17.7 us
    pallas_call x9, Pallas kernels: 29.2 us -> 24.7 us  [call(): pl.pallas_call(kernel, out_shape=[space(shape, dtype) for shape, dtype, s...]
    all_to_all x1, waiting for transfers between devices: 3.34 us -> 5.31 us  [on_pair(): p3 = after(exchange(second_sent), base)]
    ppermute x1, waiting for transfers between devices: 0.23 us -> 1.32 us  [on_pair(): o1 = across(p1)]
  transfers between devices with their start and end apart: 7 -> 7, of which waited for: 5 -> 5; matrix products, arithmetic and copies ran while one was open for 1% -> 1% of each run, Pallas kernels for 22% -> 19%
where the time goes in v1:
time: 87.1 us; the launch traced here: 85.7 us
  blocking collectives  31.8 us (37%)
  Pallas kernels  24.7 us (28%)
  waiting for transfers between devices  17.7 us (20%)
  starting transfers between devices  7.72 us (9%)
  other arithmetic  1.61 us (2%)
  local copies, waits for them, and re-layouts  1.38 us (2%)
    pallas_call x9, Pallas kernels, call(): pl.pallas_call(kernel, out_shape=[space(shape, dtype) for shape, dtype, s...  24.7 us
    all_to_all x1, blocking collectives, on_pair(): p2 = exchange(first_sent)  18.3 us
    all_to_all x1, blocking collectives, on_pair(): wanted = exchange(jnp.broadcast_to(needed, (n_row, LANES)))  13.5 us
    all_to_all x1, waiting for transfers between devices, on_pair(): p1 = after(exchange(sent), plan)  7.57 us
    all_to_all x1, waiting for transfers between devices, on_pair(): p3 = after(exchange(second_sent), base)  5.31 us
    all_to_all x1, starting transfers between devices, on_pair(): p3 = after(exchange(second_sent), base)  3.65 us
    all_to_all x1, starting transfers between devices, on_pair(): p1 = after(exchange(sent), plan)  3.51 us
    ppermute x1, waiting for transfers between devices, on_pair(): o2 = across(p2)  1.91 us
  transfers between devices with their start and end apart: 7, of which 5 were waited for; matrix products, arithmetic and copies ran while one was open for 1% of the time, Pallas kernels for 19%

profile of v1, /device:TPU:0, one launch (start us, length us, event | category | flops | bytes accessed | tf_op | source)
XLA Modules:
  0.0 85.7 jit_solution(12887532891128223053)
XLA Ops:
  0.0 0.7 and_select_fusion.1
  0.7 0.1 select_reduce_fusion
  0.9 13.5 %all_to_all.23 = s32[8,1,128]{2,1,0:T(1,128)S(1)} all-to-all(s32[8,1,128]{2,1,0:T(1,128)S(1)} %broadcast_in_dim.21), channel_id=1, replica_groups=mesh['row'=8,'col'=2,'vec'=2] {'row'}, dimensions={0} | all-to-all | bytes 8192 | tf_op jit(solution)/shard_map/all_to_all | solution.py:347
  14.4 2.4 %pick.1.picked = bf16[8,256,128]{2,1,0:T(8,128)(2,1)} custom-call(s32[8,128]{1,0:T(8,128)S(1)} %bitcast.16, bf16[8192,128]{1,0:T(8,128)(2,1)} %vectors.3), custom_call_target="tpu_custom_call" | custom-call | tf_op jit(solution)/shard_map/pick/pallas_call | solution.py:303
  16.9 3.5 %all-to-all-start.1 = ((bf16[8,256,128]{2,1,0:T(8,128)(2,1)}), bf16[8,256,128]{2,1,0:T(8,128)(2,1)S(1)}, u32[]{:S(2)}, u32[]{:S(2)}) async-start(bf16[8,256,128]{2,1,0:T(8,128)(2,1)} %pick.1.picked), calls=%async_computation.1 | async-start | bytes 1048576 | tf_op jit(solution)/shard_map/all_to_all | solution.py:445
  21.1 0.8 pad_add_fusion.1
  21.8 0.5 collective-permute-start
  22.4 1.6 %collective-permute-done.meta_b = s32[65]{0:T(128)S(1)} collective-permute-done((s32[65]{0:T(128)S(1)}, s32[65]{0:T(128)S(1)}, u32[]{:S(2)}, u32[]{:S(2)}) %collective-permute-start) | collective-permute-done | bytes 292 | tf_op jit(solution)/shard_map/ppermute | solution.py:359
  24.0 0.7 copy-done
  24.7 0.7 copy-done.1
  25.3 2.9 %plan.1 = s32[897]{0:T(1024)S(4)} custom-call(s32[2]{0:T(128)S(1)} %pad_add_fusion.place, s32[8,128]{1,0:T(8,128)S(1)} %bitcast.17, s32[32]{0:T(128)S(1)} %bitcast.21, s32[32]{0:T(128)S(1)} %bitcast.19, s32[1]{0:T(128)} %bitcast.15.used_a, s32[65]{0:T(128)S(1)} %collective-permute-done.meta_b), custom_call_target="tpu_custom_call" | custom-call | tf_op jit(solution)/shard_map/plan/pallas_call | solution.py:303
  28.2 7.6 %all-to-all-done.1.pieces.p1 = bf16[8,256,128]{2,1,0:T(8,128)(2,1)S(1)} async-done(((bf16[8,256,128]{2,1,0:T(8,128)(2,1)}), bf16[8,256,128]{2,1,0:T(8,128)(2,1)S(1)}, u32[]{:S(2)}, u32[]{:S(2)}) %all-to-all-start.1) | async-done | bytes 524320 | tf_op jit(solution)/shard_map/all_to_all | solution.py:445
  35.8 0.6 load.3.blocks
  36.4 1.3 %collective-permute-done.2.others.o1 = bf16[8,256,128]{2,1,0:T(8,128)(2,1)S(1)} collective-permute-done((bf16[8,256,128]{2,1,0:T(8,128)(2,1)S(1)}, bf16[8,256,128]{2,1,0:T(8,128)(2,1)S(1)}, u32[]{:S(2)}, u32[]{:S(2)}) %collective-permute-start.2) | collective-permute-done | bytes 524320 | tf_op jit(solution)/shard_map/ppermute | solution.py:446
  37.7 1.2 %sent.2.rest_0_ = bf16[8,256,128]{2,1,0:T(8,128)(2,1)S(1)} custom-call(s32[897]{0:T(1024)S(4)} %plan.1, bf16[64,256,256]{2,1,0:T(8,128)(2,1)S(1)} %load.3.blocks, bf16[8,256,128]{2,1,0:T(8,128)(2,1)S(1)} %all-to-all-done.1.pieces.p1, bf16[8,256,128]{2,1,0:T(8,128)(2,1)S(1)} %collective-permute-done.2.others.o1, bf16[8,256,128]{2,1,0:T(8,128)(2,1)} %pick.1.picked), custom_call_target="tpu_custom_call" | custom-call | flops 134217728 | bytes 2621440 | tf_op jit(solution)/shard_map/sent/pallas_call | solution.py:303
  38.9 18.3 %all_to_all.24.pieces.p2 = bf16[8,256,128]{2,1,0:T(8,128)(2,1)S(1)} all-to-all(bf16[8,256,128]{2,1,0:T(8,128)(2,1)S(1)} %sent.2.rest_0_), channel_id=1, replica_groups=mesh['row'=8,'col'=2,'vec'=2] {'row'}, dimensions={0} | all-to-all | bytes 1048576 | tf_op jit(solution)/shard_map/all_to_all | solution.py:449
  57.2 1.9 %collective-permute-done.3.others.o2 = bf16[8,256,128]{2,1,0:T(8,128)(2,1)S(1)} collective-permute-done((bf16[8,256,128]{2,1,0:T(8,128)(2,1)S(1)}, bf16[8,256,128]{2,1,0:T(8,128)(2,1)S(1)}, u32[]{:S(2)}, u32[]{:S(2)}) %collective-permute-start.3) | collective-permute-done | bytes 524320 | tf_op jit(solution)/shard_map/ppermute | solution.py:450
  59.1 1.9 %sent.3 = bf16[8,256,128]{2,1,0:T(8,128)(2,1)} custom-call(s32[897]{0:T(1024)S(4)} %plan.1, bf16[64,256,256]{2,1,0:T(8,128)(2,1)S(1)} %load.3.blocks, bf16[8,256,128]{2,1,0:T(8,128)(2,1)S(1)} %all_to_all.24.pieces.p2, bf16[8,256,128]{2,1,0:T(8,128)(2,1)S(1)} %collective-permute-done.3.others.o2, bf16[8,256,128]{2,1,0:T(8,128)(2,1)} %pick.1.picked, ...), custom_call_target="tpu_custom_call" | custom-call | flops 134217728 | bytes 2621440 | tf_op jit(solution)/shard_map/sent/pallas_call | solution.py:303
  61.1 3.6 %all-to-all-start.3 = ((bf16[8,256,128]{2,1,0:T(8,128)(2,1)}), bf16[8,256,128]{2,1,0:T(8,128)(2,1)S(1)}, u32[]{:S(2)}, u32[]{:S(2)}) async-start(bf16[8,256,128]{2,1,0:T(8,128)(2,1)} %sent.3), calls=%async_computation.3 | async-start | bytes 1048576 | tf_op jit(solution)/shard_map/all_to_all | solution.py:454
  64.7 2.5 %load.4.blocks = bf16[64,256,256]{2,1,0:T(8,128)(2,1)S(1)} custom-call(s32[897]{0:T(1024)S(4)} %plan.1, bf16[32,256,256]{2,1,0:T(8,128)(2,1)} %bitcast.24, bf16[32,256,256]{2,1,0:T(8,128)(2,1)} %collective-permute-done.1.tile_b), custom_call_target="tpu_custom_call" | custom-call | tf_op jit(solution)/shard_map/load/pallas_call | solution.py:303
  67.2 7.0 %early.1.array = bf16[32,256,128]{2,1,0:T(8,128)(2,1)} custom-call(s32[897]{0:T(1024)S(4)} %plan.1, bf16[64,256,256]{2,1,0:T(8,128)(2,1)S(1)} %load.4.blocks, bf16[8,256,128]{2,1,0:T(8,128)(2,1)S(1)} %all-to-all-done.1.pieces.p1, bf16[8,256,128]{2,1,0:T(8,128)(2,1)S(1)} %all_to_all.24.pieces.p2, bf16[8,256,128]{2,1,0:T(8,128)(2,1)S(1)} %collective-permute-done.2.others.o1, ...), custom_call_target="tpu_custom_call" | custom-call | flops 1073741824 | bytes 20971520 | tf_op jit(solution)/shard_map/early/pallas_call | solution.py:303
  74.2 5.3 %all-to-all-done.3.pieces = bf16[8,256,128]{2,1,0:T(8,128)(2,1)S(1)} async-done(((bf16[8,256,128]{2,1,0:T(8,128)(2,1)}), bf16[8,256,128]{2,1,0:T(8,128)(2,1)S(1)}, u32[]{:S(2)}, u32[]{:S(2)}) %all-to-all-start.3) | async-done | bytes 524320 | tf_op jit(solution)/shard_map/all_to_all | solution.py:454
  79.6 3.1 %load.5 = (bf16[64,256,256]{2,1,0:T(8,128)(2,1)S(1)}, bf16[32,256,128]{2,1,0:T(8,128)(2,1)S(1)}) custom-call(s32[897]{0:T(1024)S(4)} %plan.1, bf16[32,256,256]{2,1,0:T(8,128)(2,1)} %bitcast.25, bf16[32,256,256]{2,1,0:T(8,128)(2,1)} %collective-permute-done.1.tile_b, bf16[32,256,128]{2,1,0:T(8,128)(2,1)} %early.1.array), custom_call_target="tpu_custom_call" | custom-call | tf_op jit(solution)/shard_map/load/pallas_call | solution.py:303
  82.6 3.0 %last.1 = bf16[32,256,128]{2,1,0:T(8,128)(2,1)} custom-call(s32[897]{0:T(1024)S(4)} %plan.1, bf16[64,256,256]{2,1,0:T(8,128)(2,1)S(1)} %get-tuple-element.21.blocks, bf16[8,256,128]{2,1,0:T(8,128)(2,1)S(1)} %all-to-all-done.3.pieces, bf16[8,256,128]{2,1,0:T(8,128)(2,1)S(1)} %collective-permute-done.4.others, bf16[32,256,128]{2,1,0:T(8,128)(2,1)S(1)} %get-tuple-element.22.base), custom_call_target="tpu_custom_call" | custom-call | flops 536870912 | bytes 10485760 | tf_op jit(solution)/shard_map/last/pallas_call | solution.py:303
  (10 shorter events, 0.2 us)
Async XLA Ops:
  16.8 19.0 %collective-permute-start.1 = (bf16[32,256,256]{2,1,0:T(8,128)(2,1)}, bf16[32,256,256]{2,1,0:T(8,128)(2,1)}, u32[]{:S(2)}, u32[]{:S(2)}) collective-permute-start(bf16[32,256,256]{2,1,0:T(8,128)(2,1)} %bitcast.22), channel_id=1, source_target_pairs={{0,2},{2,0},{1,3},{3,1},{4,6},{6,4},{5,7},{7,5},{8,10},{10,8},{9,1... | collective-permute-start | bytes 12582920 | tf_op jit(solution)/shard_map/ppermute | solution.py:358
  16.9 18.9 %all-to-all-start.1 = ((bf16[8,256,128]{2,1,0:T(8,128)(2,1)}), bf16[8,256,128]{2,1,0:T(8,128)(2,1)S(1)}, u32[]{:S(2)}, u32[]{:S(2)}) async-start(bf16[8,256,128]{2,1,0:T(8,128)(2,1)} %pick.1.picked), calls=%async_computation.1 | async-start | bytes 1048576 | tf_op jit(solution)/shard_map/all_to_all | solution.py:445
  21.8 2.2 %collective-permute-start = (s32[65]{0:T(128)S(1)}, s32[65]{0:T(128)S(1)}, u32[]{:S(2)}, u32[]{:S(2)}) collective-permute-start(s32[65]{0:T(128)S(1)} %pad_add_fusion.1), channel_id=1, source_target_pairs={{0,2},{2,0},{1,3},{3,1},{4,6},{6,4},{5,7},{7,5},{8,10},{10,8},{9,1... | collective-permute-start | bytes 788 | tf_op jit(solution)/shard_map/ppermute | solution.py:359
  24.0 0.7 copy-start
  24.7 0.7 copy-start.1
  35.8 1.9 %collective-permute-start.2 = (bf16[8,256,128]{2,1,0:T(8,128)(2,1)S(1)}, bf16[8,256,128]{2,1,0:T(8,128)(2,1)S(1)}, u32[]{:S(2)}, u32[]{:S(2)}) collective-permute-start(bf16[8,256,128]{2,1,0:T(8,128)(2,1)S(1)} %all-to-all-done.1.pieces.p1), channel_id=1, source_target_pairs={{0,2},{2,0},{1,3},{3,1},{4,6},{6,4},{5,7},{7,5},{8,10},{10,8},{9,1... | collective-permute-start | bytes 1572872 | tf_op jit(solution)/shard_map/ppermute | solution.py:446
  57.2 1.9 %collective-permute-start.3 = (bf16[8,256,128]{2,1,0:T(8,128)(2,1)S(1)}, bf16[8,256,128]{2,1,0:T(8,128)(2,1)S(1)}, u32[]{:S(2)}, u32[]{:S(2)}) collective-permute-start(bf16[8,256,128]{2,1,0:T(8,128)(2,1)S(1)} %all_to_all.24.pieces.p2), channel_id=1, source_target_pairs={{0,2},{2,0},{1,3},{3,1},{4,6},{6,4},{5,7},{7,5},{8,10},{10,8},{9,1... | collective-permute-start | bytes 1572872 | tf_op jit(solution)/shard_map/ppermute | solution.py:450
  61.1 18.5 %all-to-all-start.3 = ((bf16[8,256,128]{2,1,0:T(8,128)(2,1)}), bf16[8,256,128]{2,1,0:T(8,128)(2,1)S(1)}, u32[]{:S(2)}, u32[]{:S(2)}) async-start(bf16[8,256,128]{2,1,0:T(8,128)(2,1)} %sent.3), calls=%async_computation.3 | async-start | bytes 1048576 | tf_op jit(solution)/shard_map/all_to_all | solution.py:454
  79.6 3.1 %collective-permute-start.4 = (bf16[8,256,128]{2,1,0:T(8,128)(2,1)S(1)}, bf16[8,256,128]{2,1,0:T(8,128)(2,1)S(1)}, u32[]{:S(2)}, u32[]{:S(2)}) collective-permute-start(bf16[8,256,128]{2,1,0:T(8,128)(2,1)S(1)} %all-to-all-done.3.pieces), channel_id=1, source_target_pairs={{0,2},{2,0},{1,3},{3,1},{4,6},{6,4},{5,7},{7,5},{8,10},{10,8},{9,1... | collective-permute-start | bytes 1572872 | tf_op jit(solution)/shard_map/ppermute | solution.py:455

commit v2 on v1

--- a/solution.py
+++ b/solution.py
@@ -17,7 +17,7 @@
 HBM = pltpu.HBM
 DMA = pltpu.SemaphoreType.DMA
 LANES = 128
-FEW = 2
+FEW = 4
 MANY = 4
 HEAD = 8
 STRIDE = 4
@@ -355,7 +355,7 @@
         2,
         "pick",
     )
-    tile_other = across(after(tile, sent))
+    tile_other = across(tile)
     meta = across(after(jnp.concatenate([slot_rows, slot_cols, used]), sent))
 
     capacity = 2 * round_up(slot_count, MANY)

time: 87.1 us -> 84 us (0.964)
  the two profiles are of different devices: /device:TPU:0 before, /device:TPU:3 now
where the time goes in v2:
time: 84 us; the launch traced here: 83.4 us
  Pallas kernels  26.9 us (32%)
  blocking collectives  26.1 us (31%)
  starting transfers between devices  15.2 us (18%)
  waiting for transfers between devices  11.4 us (14%)
  other arithmetic  1.61 us (2%)
  local copies, waits for them, and re-layouts  1.38 us (2%)
    pallas_call x9, Pallas kernels, call(): pl.pallas_call(kernel, out_shape=[space(shape, dtype) for shape, dtype, s...  26.9 us
    all_to_all x1, blocking collectives, on_pair(): p2 = exchange(first_sent)  16.4 us
    all_to_all x1, blocking collectives, on_pair(): wanted = exchange(jnp.broadcast_to(needed, (n_row, LANES)))  9.69 us
    all_to_all x1, waiting for transfers between devices, on_pair(): p1 = after(exchange(sent), plan)  4.87 us
    all_to_all x1, starting transfers between devices, on_pair(): p1 = after(exchange(sent), plan)  4.6 us
    all_to_all x1, waiting for transfers between devices, on_pair(): p3 = after(exchange(second_sent), base)  4.21 us
    all_to_all x1, starting transfers between devices, on_pair(): p3 = after(exchange(second_sent), base)  3.46 us
    ppermute x1, starting transfers between devices, on_pair(): meta = across(after(jnp.concatenate([slot_rows, slot_cols, used]), sent))  1.71 us
  transfers between devices with their start and end apart: 7, of which 4 were waited for; matrix products, arithmetic and copies ran while one was open for 2% of the time, Pallas kernels for 24%

profile of v2, /device:TPU:3, one launch (start us, length us, event | category | flops | bytes accessed | tf_op | source)
XLA Modules:
  0.0 83.4 jit_solution(6342226125045991855)
XLA Ops:
  0.0 0.7 collective-permute-start.1
  0.7 0.7 and_select_fusion.1
  1.5 9.7 %all_to_all.23 = s32[8,1,128]{2,1,0:T(1,128)S(1)} all-to-all(s32[8,1,128]{2,1,0:T(1,128)S(1)} %broadcast_in_dim.21), channel_id=1, replica_groups=mesh['row'=8,'col'=2,'vec'=2] {'row'}, dimensions={0} | all-to-all | bytes 8192 | tf_op jit(solution)/shard_map/all_to_all | solution.py:347
  11.2 2.4 %pick.1.picked = bf16[8,256,128]{2,1,0:T(8,128)(2,1)} custom-call(s32[8,128]{1,0:T(8,128)S(1)} %bitcast.16, bf16[8192,128]{1,0:T(8,128)(2,1)} %vectors.3), custom_call_target="tpu_custom_call" | custom-call | tf_op jit(solution)/shard_map/pick/pallas_call | solution.py:303
  13.7 4.6 %all-to-all-start.1 = ((bf16[8,256,128]{2,1,0:T(8,128)(2,1)}), bf16[8,256,128]{2,1,0:T(8,128)(2,1)S(1)}, u32[]{:S(2)}, u32[]{:S(2)}) async-start(bf16[8,256,128]{2,1,0:T(8,128)(2,1)} %pick.1.picked), calls=%async_computation.1 | async-start | bytes 1048576 | tf_op jit(solution)/shard_map/all_to_all | solution.py:445
  18.9 0.8 pad_add_fusion.1
  19.7 1.7 %collective-permute-start = (s32[65]{0:T(128)S(1)}, s32[65]{0:T(128)S(1)}, u32[]{:S(2)}, u32[]{:S(2)}) collective-permute-start(s32[65]{0:T(128)S(1)} %pad_add_fusion.1), channel_id=1, source_target_pairs={{0,2},{2,0},{1,3},{3,1},{4,6},{6,4},{5,7},{7,5},{8,10},{10,8},{9,1... | collective-permute-start | bytes 788 | tf_op jit(solution)/shard_map/ppermute | solution.py:359
  21.5 0.7 collective-permute-done.meta_b
  23.5 3.4 %plan.1 = s32[913]{0:T(1024)S(4)} custom-call(s32[2]{0:T(128)S(1)} %pad_add_fusion.place, s32[8,128]{1,0:T(8,128)S(1)} %bitcast.17, s32[32]{0:T(128)S(1)} %bitcast.21, s32[32]{0:T(128)S(1)} %bitcast.19, s32[1]{0:T(128)} %bitcast.15.used_a, s32[65]{0:T(128)S(1)} %collective-permute-done.meta_b), custom_call_target="tpu_custom_call" | custom-call | tf_op jit(solution)/shard_map/plan/pallas_call | solution.py:303
  26.9 4.9 %all-to-all-done.1.pieces.p1 = bf16[8,256,128]{2,1,0:T(8,128)(2,1)S(1)} async-done(((bf16[8,256,128]{2,1,0:T(8,128)(2,1)}), bf16[8,256,128]{2,1,0:T(8,128)(2,1)S(1)}, u32[]{:S(2)}, u32[]{:S(2)}) %all-to-all-start.1) | async-done | bytes 524320 | tf_op jit(solution)/shard_map/all_to_all | solution.py:445
  31.8 1.7 %collective-permute-start.2 = (bf16[8,256,128]{2,1,0:T(8,128)(2,1)S(1)}, bf16[8,256,128]{2,1,0:T(8,128)(2,1)S(1)}, u32[]{:S(2)}, u32[]{:S(2)}) collective-permute-start(bf16[8,256,128]{2,1,0:T(8,128)(2,1)S(1)} %all-to-all-done.1.pieces.p1), channel_id=1, source_target_pairs={{0,2},{2,0},{1,3},{3,1},{4,6},{6,4},{5,7},{7,5},{8,10},{10,8},{9,1... | collective-permute-start | bytes 1572872 | tf_op jit(solution)/shard_map/ppermute | solution.py:446
  33.5 1.8 %load.3.blocks = bf16[64,256,256]{2,1,0:T(8,128)(2,1)S(1)} custom-call(s32[913]{0:T(1024)S(4)} %plan.1, bf16[32,256,256]{2,1,0:T(8,128)(2,1)} %bitcast.23, bf16[32,256,256]{2,1,0:T(8,128)(2,1)} %collective-permute-done.1.tile_b), custom_call_target="tpu_custom_call" | custom-call | tf_op jit(solution)/shard_map/load/pallas_call | solution.py:303
  35.3 1.4 %sent.2.rest_0_ = bf16[8,256,128]{2,1,0:T(8,128)(2,1)S(1)} custom-call(s32[913]{0:T(1024)S(4)} %plan.1, bf16[64,256,256]{2,1,0:T(8,128)(2,1)S(1)} %load.3.blocks, bf16[8,256,128]{2,1,0:T(8,128)(2,1)S(1)} %all-to-all-done.1.pieces.p1, bf16[8,256,128]{2,1,0:T(8,128)(2,1)S(1)} %collective-permute-done.2.others.o1, bf16[8,256,128]{2,1,0:T(8,128)(2,1)} %pick.1.picked), custom_call_target="tpu_custom_call" | custom-call | flops 134217728 | bytes 2621440 | tf_op jit(solution)/shard_map/sent/pallas_call | solution.py:303
  36.7 16.4 %all_to_all.24.pieces.p2 = bf16[8,256,128]{2,1,0:T(8,128)(2,1)S(1)} all-to-all(bf16[8,256,128]{2,1,0:T(8,128)(2,1)S(1)} %sent.2.rest_0_), channel_id=1, replica_groups=mesh['row'=8,'col'=2,'vec'=2] {'row'}, dimensions={0} | all-to-all | bytes 1048576 | tf_op jit(solution)/shard_map/all_to_all | solution.py:449
  53.1 1.7 %collective-permute-start.3 = (bf16[8,256,128]{2,1,0:T(8,128)(2,1)S(1)}, bf16[8,256,128]{2,1,0:T(8,128)(2,1)S(1)}, u32[]{:S(2)}, u32[]{:S(2)}) collective-permute-start(bf16[8,256,128]{2,1,0:T(8,128)(2,1)S(1)} %all_to_all.24.pieces.p2), channel_id=1, source_target_pairs={{0,2},{2,0},{1,3},{3,1},{4,6},{6,4},{5,7},{7,5},{8,10},{10,8},{9,1... | collective-permute-start | bytes 1572872 | tf_op jit(solution)/shard_map/ppermute | solution.py:450
  54.8 1.5 %collective-permute-done.3.others.o2 = bf16[8,256,128]{2,1,0:T(8,128)(2,1)S(1)} collective-permute-done((bf16[8,256,128]{2,1,0:T(8,128)(2,1)S(1)}, bf16[8,256,128]{2,1,0:T(8,128)(2,1)S(1)}, u32[]{:S(2)}, u32[]{:S(2)}) %collective-permute-start.3) | collective-permute-done | bytes 524320 | tf_op jit(solution)/shard_map/ppermute | solution.py:450
  56.4 2.2 %sent.3 = bf16[8,256,128]{2,1,0:T(8,128)(2,1)} custom-call(s32[913]{0:T(1024)S(4)} %plan.1, bf16[64,256,256]{2,1,0:T(8,128)(2,1)S(1)} %load.3.blocks, bf16[8,256,128]{2,1,0:T(8,128)(2,1)S(1)} %all_to_all.24.pieces.p2, bf16[8,256,128]{2,1,0:T(8,128)(2,1)S(1)} %collective-permute-done.3.others.o2, bf16[8,256,128]{2,1,0:T(8,128)(2,1)} %pick.1.picked, ...), custom_call_target="tpu_custom_call" | custom-call | flops 134217728 | bytes 2621440 | tf_op jit(solution)/shard_map/sent/pallas_call | solution.py:303
  58.5 3.5 %all-to-all-start.3 = ((bf16[8,256,128]{2,1,0:T(8,128)(2,1)}), bf16[8,256,128]{2,1,0:T(8,128)(2,1)S(1)}, u32[]{:S(2)}, u32[]{:S(2)}) async-start(bf16[8,256,128]{2,1,0:T(8,128)(2,1)} %sent.3), calls=%async_computation.3 | async-start | bytes 1048576 | tf_op jit(solution)/shard_map/all_to_all | solution.py:454
  62.0 2.5 %load.4.blocks = bf16[64,256,256]{2,1,0:T(8,128)(2,1)S(1)} custom-call(s32[913]{0:T(1024)S(4)} %plan.1, bf16[32,256,256]{2,1,0:T(8,128)(2,1)} %bitcast.24, bf16[32,256,256]{2,1,0:T(8,128)(2,1)} %collective-permute-done.1.tile_b), custom_call_target="tpu_custom_call" | custom-call | tf_op jit(solution)/shard_map/load/pallas_call | solution.py:303
  64.5 7.0 %early.1.array = bf16[32,256,128]{2,1,0:T(8,128)(2,1)} custom-call(s32[913]{0:T(1024)S(4)} %plan.1, bf16[64,256,256]{2,1,0:T(8,128)(2,1)S(1)} %load.4.blocks, bf16[8,256,128]{2,1,0:T(8,128)(2,1)S(1)} %all-to-all-done.1.pieces.p1, bf16[8,256,128]{2,1,0:T(8,128)(2,1)S(1)} %all_to_all.24.pieces.p2, bf16[8,256,128]{2,1,0:T(8,128)(2,1)S(1)} %collective-permute-done.2.others.o1, ...), custom_call_target="tpu_custom_call" | custom-call | flops 1073741824 | bytes 20971520 | tf_op jit(solution)/shard_map/early/pallas_call | solution.py:303
  71.6 4.2 %all-to-all-done.3.pieces = bf16[8,256,128]{2,1,0:T(8,128)(2,1)S(1)} async-done(((bf16[8,256,128]{2,1,0:T(8,128)(2,1)}), bf16[8,256,128]{2,1,0:T(8,128)(2,1)S(1)}, u32[]{:S(2)}, u32[]{:S(2)}) %all-to-all-start.3) | async-done | bytes 524320 | tf_op jit(solution)/shard_map/all_to_all | solution.py:454
  75.8 1.4 %collective-permute-start.4 = (bf16[8,256,128]{2,1,0:T(8,128)(2,1)S(1)}, bf16[8,256,128]{2,1,0:T(8,128)(2,1)S(1)}, u32[]{:S(2)}, u32[]{:S(2)}) collective-permute-start(bf16[8,256,128]{2,1,0:T(8,128)(2,1)S(1)} %all-to-all-done.3.pieces), channel_id=1, source_target_pairs={{0,2},{2,0},{1,3},{3,1},{4,6},{6,4},{5,7},{7,5},{8,10},{10,8},{9,1... | collective-permute-start | bytes 1572872 | tf_op jit(solution)/shard_map/ppermute | solution.py:455
  77.2 3.0 %load.5 = (bf16[64,256,256]{2,1,0:T(8,128)(2,1)S(1)}, bf16[32,256,128]{2,1,0:T(8,128)(2,1)S(1)}) custom-call(s32[913]{0:T(1024)S(4)} %plan.1, bf16[32,256,256]{2,1,0:T(8,128)(2,1)} %bitcast.25, bf16[32,256,256]{2,1,0:T(8,128)(2,1)} %collective-permute-done.1.tile_b, bf16[32,256,128]{2,1,0:T(8,128)(2,1)} %early.1.array), custom_call_target="tpu_custom_call" | custom-call | tf_op jit(solution)/shard_map/load/pallas_call | solution.py:303
  80.2 3.1 %last.1 = bf16[32,256,128]{2,1,0:T(8,128)(2,1)} custom-call(s32[913]{0:T(1024)S(4)} %plan.1, bf16[64,256,256]{2,1,0:T(8,128)(2,1)S(1)} %get-tuple-element.19.blocks, bf16[8,256,128]{2,1,0:T(8,128)(2,1)S(1)} %all-to-all-done.3.pieces, bf16[8,256,128]{2,1,0:T(8,128)(2,1)S(1)} %collective-permute-done.4.others, bf16[32,256,128]{2,1,0:T(8,128)(2,1)S(1)} %get-tuple-element.20.base), custom_call_target="tpu_custom_call" | custom-call | flops 536870912 | bytes 10485760 | tf_op jit(solution)/shard_map/last/pallas_call | solution.py:303
  (10 shorter events, 1.6 us)
Async XLA Ops:
  0.0 33.5 %collective-permute-start.1 = (bf16[32,256,256]{2,1,0:T(8,128)(2,1)}, bf16[32,256,256]{2,1,0:T(8,128)(2,1)}, u32[]{:S(2)}, u32[]{:S(2)}) collective-permute-start(bf16[32,256,256]{2,1,0:T(8,128)(2,1)} %bitcast.22), channel_id=1, source_target_pairs={{0,2},{2,0},{1,3},{3,1},{4,6},{6,4},{5,7},{7,5},{8,10},{10,8},{9,1... | collective-permute-start | bytes 12582920 | tf_op jit(solution)/shard_map/ppermute | solution.py:358
  13.7 18.1 %all-to-all-start.1 = ((bf16[8,256,128]{2,1,0:T(8,128)(2,1)}), bf16[8,256,128]{2,1,0:T(8,128)(2,1)S(1)}, u32[]{:S(2)}, u32[]{:S(2)}) async-start(bf16[8,256,128]{2,1,0:T(8,128)(2,1)} %pick.1.picked), calls=%async_computation.1 | async-start | bytes 1048576 | tf_op jit(solution)/shard_map/all_to_all | solution.py:445
  19.7 2.5 %collective-permute-start = (s32[65]{0:T(128)S(1)}, s32[65]{0:T(128)S(1)}, u32[]{:S(2)}, u32[]{:S(2)}) collective-permute-start(s32[65]{0:T(128)S(1)} %pad_add_fusion.1), channel_id=1, source_target_pairs={{0,2},{2,0},{1,3},{3,1},{4,6},{6,4},{5,7},{7,5},{8,10},{10,8},{9,1... | collective-permute-start | bytes 788 | tf_op jit(solution)/shard_map/ppermute | solution.py:359
  22.2 0.7 copy-start
  22.9 0.7 copy-start.1
  31.8 3.5 %collective-permute-start.2 = (bf16[8,256,128]{2,1,0:T(8,128)(2,1)S(1)}, bf16[8,256,128]{2,1,0:T(8,128)(2,1)S(1)}, u32[]{:S(2)}, u32[]{:S(2)}) collective-permute-start(bf16[8,256,128]{2,1,0:T(8,128)(2,1)S(1)} %all-to-all-done.1.pieces.p1), channel_id=1, source_target_pairs={{0,2},{2,0},{1,3},{3,1},{4,6},{6,4},{5,7},{7,5},{8,10},{10,8},{9,1... | collective-permute-start | bytes 1572872 | tf_op jit(solution)/shard_map/ppermute | solution.py:446
  53.1 3.2 %collective-permute-start.3 = (bf16[8,256,128]{2,1,0:T(8,128)(2,1)S(1)}, bf16[8,256,128]{2,1,0:T(8,128)(2,1)S(1)}, u32[]{:S(2)}, u32[]{:S(2)}) collective-permute-start(bf16[8,256,128]{2,1,0:T(8,128)(2,1)S(1)} %all_to_all.24.pieces.p2), channel_id=1, source_target_pairs={{0,2},{2,0},{1,3},{3,1},{4,6},{6,4},{5,7},{7,5},{8,10},{10,8},{9,1... | collective-permute-start | bytes 1572872 | tf_op jit(solution)/shard_map/ppermute | solution.py:450
  58.5 17.2 %all-to-all-start.3 = ((bf16[8,256,128]{2,1,0:T(8,128)(2,1)}), bf16[8,256,128]{2,1,0:T(8,128)(2,1)S(1)}, u32[]{:S(2)}, u32[]{:S(2)}) async-start(bf16[8,256,128]{2,1,0:T(8,128)(2,1)} %sent.3), calls=%async_computation.3 | async-start | bytes 1048576 | tf_op jit(solution)/shard_map/all_to_all | solution.py:454
  75.8 4.5 %collective-permute-start.4 = (bf16[8,256,128]{2,1,0:T(8,128)(2,1)S(1)}, bf16[8,256,128]{2,1,0:T(8,128)(2,1)S(1)}, u32[]{:S(2)}, u32[]{:S(2)}) collective-permute-start(bf16[8,256,128]{2,1,0:T(8,128)(2,1)S(1)} %all-to-all-done.3.pieces), channel_id=1, source_target_pairs={{0,2},{2,0},{1,3},{3,1},{4,6},{6,4},{5,7},{7,5},{8,10},{10,8},{9,1... | collective-permute-start | bytes 1572872 | tf_op jit(solution)/shard_map/ppermute | solution.py:455

commit v3 on v2

--- a/solution.py
+++ b/solution.py
@@ -38,17 +38,30 @@
 
 
 def plan_kernel(
-    n_row, piece_blocks, sent_at, load_at, bare_at, place, wanted, rows_a, cols_a, used_a, meta_b, out, seen
+    n_row,
+    piece_blocks,
+    sent_at,
+    load_at,
+    bare_at,
+    place,
+    wanted_a,
+    wanted_b,
+    rows_a,
+    cols_a,
+    used_a,
+    meta_b,
+    out,
+    seen,
 ):
     slot_count = rows_a.shape[0]
-    first_row = place[1] * piece_blocks
+    own_half = place[1]
 
     def scan(row_of, col_of, used, at, sent, load):
         def step(s, carry):
             at, sent, load = carry
-            row = row_of(s) - first_row
-            inside = (row >= 0) & (row < piece_blocks)
-            mine = inside.astype(jnp.int32)
+            half = row_of(s) // piece_blocks
+            row = row_of(s) - half * piece_blocks
+            inside = half == own_half
             piece = col_of(s) // piece_blocks
             kept = jnp.where(inside, row, piece_blocks)
             entry = HEAD + STRIDE * at
@@ -61,14 +74,15 @@
             before = sent
             for k in range(n_row):
                 out[sent_at + STRIDE * sent] = load
-                out[sent_at + STRIDE * sent + 1] = k
+                out[sent_at + STRIDE * sent + 1] = 2 * k + half
                 out[sent_at + STRIDE * sent + 2] = piece
-                sent = sent + jnp.where(wanted[k, 0] == row, mine, 0)
-            return at + mine, sent, load + (sent > before).astype(jnp.int32)
+                asked = jnp.where(inside, wanted_a[k, 0], wanted_b[k, 0])
+                sent = sent + (asked == row).astype(jnp.int32)
+            return at + inside.astype(jnp.int32), sent, load + (sent > before).astype(jnp.int32)
 
         at, sent, load = lax.fori_loop(0, used, step, (at, sent, load))
         for _ in range(MANY):
-            for base, end, spare in ((HEAD, at, piece_blocks), (sent_at, sent, n_row)):
+            for base, end, spare in ((HEAD, at, piece_blocks), (sent_at, sent, 2 * n_row)):
                 entry = base + STRIDE * end
                 out[entry] = 0
                 out[entry + 1] = spare
@@ -110,6 +124,7 @@
         return bare + jnp.where(entry == 0, 1, 0)
 
     out[6] = lax.fori_loop(0, piece_blocks, close, zero)
+    out[7] = own_half
 
 
 def pick_kernel(n_row, block_size, wanted, vectors, out, held, in_sems, out_sems):
@@ -186,49 +201,106 @@
     each_product(plan, base, ends, blocks, pieces, use)
 
 
-def sent_kernel(first, sent_at, plan, blocks, pieces, others, picked, *rest):
-    if first:
-        out, total, held, held_sem = rest
-    else:
-        current, out, total, held, held_sem, ready, out_sems = rest
+def lanes_of(shape, half):
+    column = lax.broadcasted_iota(jnp.int32, shape, 1)
+    return (column // (shape[1] // 2)) == half
+
+
+def only_half(vec, side, pieces, half):
+    keep = jnp.where(lanes_of((1, vec.shape[-1]), half), 1.0, 0.0).astype(jnp.bfloat16)
+    for p in range(vec.shape[1]):
+        vec[side, p] = pieces[p] * keep
+
+
+def joined(total, k):
+    one, two = total[2 * k], total[2 * k + 1]
+    low = lanes_of(one.shape, 0)
+    return jnp.where(low, one, two) + pltpu.roll(
+        jnp.where(low, two, one), one.shape[1] // 2, axis=1
+    )
+
+
+def first_sent_kernel(
+    sent_at, plan, blocks, pieces, others, picked, picked_b, out, start, vec, total, held, held_sems
+):
     n_row = out.shape[0]
-    copy = pltpu.make_async_copy(picked, held, held_sem)
-    copy.start()
+    half = plan[7]
+    copies = [
+        pltpu.make_async_copy(source, held.at[i], held_sems.at[i])
+        for i, source in enumerate((picked, picked_b))
+    ]
+    for copy in copies:
+        copy.start()
+    only_half(vec, 0, pieces, half)
+    only_half(vec, 1, others, half)
+    total[...] = jnp.zeros_like(total)
+    add_products(plan, sent_at, 2, blocks, (vec.at[0], vec.at[1]), total)
+    for copy in copies:
+        copy.wait()
+    mine = lanes_of(out.shape[1:], half)
     for k in range(n_row):
-        if first:
-            total[k] = jnp.zeros(total.shape[1:], jnp.float32)
-        else:
-            total[k] = -center_value * current[k].astype(jnp.float32)
-    add_products(plan, sent_at, 2, blocks, (pieces, others), total)
-    copy.wait()
-    if first:
-        for k in range(n_row):
-            value = total[k] - center_value * held[k].astype(jnp.float32)
-            out[k] = (value / half_width).astype(jnp.bfloat16)
-        return
+        own = held[0, k].astype(jnp.float32)
+        other = pltpu.roll(held[1, k].astype(jnp.float32), out.shape[2] // 2, axis=1)
+        value = jnp.where(mine, own, other)
+        start[k] = value.astype(jnp.bfloat16)
+        out[k] = ((joined(total, k) - center_value * value) / half_width).astype(jnp.bfloat16)
+
+
+def second_sent_kernel(
+    sent_at, plan, blocks, pieces, previous, current, out, vec, total, ready, out_sems
+):
+    n_row = out.shape[0]
+    half = plan[7]
+    only_half(vec, 0, pieces, half)
+    only_half(vec, 1, pieces, 1 - half)
+    total[...] = jnp.zeros_like(total)
+    add_products(plan, sent_at, 2, blocks, (vec.at[0], vec.at[1]), total)
 
     def put(k):
         return pltpu.make_async_copy(ready.at[k], out.at[k], out_sems.at[k])
 
     for k in range(n_row):
-        ready[k] = (total[k] - held[k].astype(jnp.float32)).astype(jnp.bfloat16)
+        value = joined(total, k) - center_value * current[k].astype(jnp.float32)
+        ready[k] = (value - previous[k].astype(jnp.float32)).astype(jnp.bfloat16)
         put(k).start()
     for k in range(n_row):
         put(k).wait()
 
 
-def early_kernel(plan, blocks, p1, p2, o1, o2, vectors, base, vec, total, own, sems, row_sems):
+def whole_columns(half, mine, other, vec, at):
+    n_row, _, width = mine.shape
+    middle = width // 2
+
+    def merge(lower, upper, sides):
+        @pl.loop(0, n_row)
+        def _(p):
+            for side, column in sides:
+                part = slice(column * middle, (column + 1) * middle)
+                vec[side, p, :, at : at + middle] = lower[p, :, part]
+                vec[side, p, :, at + middle : at + width] = upper[p, :, part]
+
+    @pl.when(half == 0)
+    def _():
+        merge(mine, other, ((0, 0), (1, 1)))
+
+    @pl.when(half == 1)
+    def _():
+        merge(other, mine, ((0, 1), (1, 0)))
+
+
+def early_kernel(
+    plan, blocks, pieces, others, mine, other, vectors, base, vec, total, own, sems, row_sems
+):
     width = vectors.shape[1]
     piece_blocks, block_size, _ = base.shape
     copies = [
-        pltpu.make_async_copy(
-            source, vec.at[side, :, :, pl.ds(step * width, width)], sems.at[2 * side + step]
-        )
-        for side, step, source in ((0, 0, p1), (0, 1, p2), (1, 0, o1), (1, 1, o2))
+        pltpu.make_async_copy(source, vec.at[side, :, :, pl.ds(0, width)], sems.at[side])
+        for side, source in enumerate((pieces, others))
     ]
-    copies.append(pltpu.make_async_copy(vectors, own, sems.at[4]))
+    copies.append(pltpu.make_async_copy(vectors, own, sems.at[2]))
     for copy in copies:
         copy.start()
+    whole_columns(plan[7], mine, other, vec, width)
     copies[-1].wait()
 
     def rows(b):
@@ -260,7 +332,7 @@
         put(b).wait()
 
 
-def last_kernel(bare_at, plan, blocks, pieces, others, base, out, total, own, row_sems):
+def last_kernel(bare_at, plan, blocks, mine, other, base, out, vec, total, own, row_sems):
     piece_blocks = base.shape[0]
 
     def put(source, b):
@@ -270,6 +342,8 @@
     def _(i):
         b = plan[bare_at + i]
         put(base, b).start()
+
+    whole_columns(plan[7], mine, other, vec, 0)
 
     def use(entry, value):
         row = plan[entry + 1]
@@ -284,7 +358,7 @@
         def _():
             put(own, plan[entry + 1]).start()
 
-    each_product(plan, HEAD, 0, blocks, (pieces, others), use, then)
+    each_product(plan, HEAD, 0, blocks, (vec.at[0], vec.at[1]), use, then)
 
     @pl.loop(0, piece_blocks)
     def _(b):
@@ -356,18 +430,20 @@
         "pick",
     )
     tile_other = across(tile)
+    wanted_other = across(after(wanted, sent))
     meta = across(after(jnp.concatenate([slot_rows, slot_cols, used]), sent))
+    sent_other = across(sent)
 
     capacity = 2 * round_up(slot_count, MANY)
     sent_at = HEAD + STRIDE * (capacity + 1)
-    load_at = sent_at + STRIDE * (2 * n_row * n_row + 2 * FEW + 1)
+    load_at = sent_at + STRIDE * (4 * n_row * n_row + 2 * FEW + 1)
     bare_at = load_at + 2 * slot_count + 1
     plan_size = bare_at + piece_blocks
     (plan,) = call(
         functools.partial(plan_kernel, n_row, piece_blocks, sent_at, load_at, bare_at),
         [((plan_size,), jnp.int32, SMEM)],
-        (place, wanted, slot_rows, slot_cols, used, meta),
-        (SCALARS,) * 6,
+        (place, wanted, wanted_other, slot_rows, slot_cols, used, meta),
+        (SCALARS,) * 7,
         [SMEM((piece_blocks + 1,), jnp.int32)],
         2,
         "plan",
@@ -393,17 +469,31 @@
             transcendentals=0,
         )
 
-    def sent_blocks(blocks, *args):
-        first = len(args) == 3
-        held = [VMEM(sent_shape, jnp.bfloat16), DMA]
-        staged = [] if first else [VMEM(sent_shape, jnp.bfloat16), DMA((n_row,))]
+    sums = [
+        VMEM((2, n_row, block_size, width), jnp.bfloat16),
+        VMEM((2 * n_row + 1, block_size, width), jnp.float32),
+    ]
+
+    def first_blocks(*args):
         return call(
-            functools.partial(sent_kernel, first, sent_at),
-            [(sent_shape, jnp.bfloat16, VMEM if first else HBM)],
-            (plan, blocks, *args),
-            (LIST, HERE, HERE, HERE, FAR) + (HERE,) * (len(args) - 3),
-            [VMEM((n_row + 1, block_size, width), jnp.float32)] + held + staged,
-            4,
+            functools.partial(first_sent_kernel, sent_at),
+            [(sent_shape, jnp.bfloat16, VMEM)] * 2,
+            (plan, *args),
+            (LIST, HERE, HERE, HERE, FAR, FAR),
+            sums + [VMEM((2, *sent_shape), jnp.bfloat16), DMA((2,))],
+            8,
+            "sent",
+            cost(n_row, n_row),
+        )
+
+    def second_blocks(*args):
+        return call(
+            functools.partial(second_sent_kernel, sent_at),
+            [(sent_shape, jnp.bfloat16, HBM)],
+            (plan, *args),
+            (LIST, HERE, HERE, HERE, HERE),
+            sums + [VMEM(sent_shape, jnp.bfloat16), DMA((n_row,))],
+            8,
             "sent",
             cost(n_row, n_row),
         )[0]
@@ -420,7 +510,7 @@
                 VMEM((2, n_row, block_size, 2 * width), jnp.bfloat16),
                 VMEM((piece_blocks + 1, block_size, 2 * width), jnp.float32),
                 VMEM(vectors.shape, jnp.bfloat16),
-                DMA((5,)),
+                DMA((3,)),
                 DMA((piece_blocks,)),
             ],
             18,
@@ -435,26 +525,30 @@
             [(base_shape, jnp.bfloat16, HBM)],
             (plan, blocks, *args),
             (LIST,) + (HERE,) * 4,
-            [VMEM(rows, jnp.float32), VMEM(rows, jnp.bfloat16), DMA((piece_blocks,))],
-            8,
+            [
+                VMEM((2, n_row, block_size, width), jnp.bfloat16),
+                VMEM(rows, jnp.float32),
+                VMEM(rows, jnp.bfloat16),
+                DMA((piece_blocks,)),
+            ],
+            9,
             "last",
             cost(slot_count, piece_blocks),
         )
         return out.reshape(vectors.shape)
 
-    p1 = after(exchange(sent), plan)
+    p1 = after(exchange(sent), plan, sent_other)
     o1 = across(p1)
     (blocks,) = load(load_at, 1, 4, p1)
-    first_sent = sent_blocks(blocks, p1, o1, sent)
-    p2 = exchange(first_sent)
-    o2 = across(p2)
-    second_sent = sent_blocks(blocks, p2, o2, sent, first_sent)
+    first_sent, start = first_blocks(blocks, p1, o1, sent, sent_other)
+    q2 = exchange(first_sent)
+    second_sent = second_blocks(blocks, q2, start, first_sent)
     (blocks,) = load(HEAD, STRIDE, 0, second_sent)
-    base = early(blocks, p1, p2, o1, o2)
-    p3 = after(exchange(second_sent), base)
-    o3 = across(p3)
-    blocks, base = load(HEAD, STRIDE, 0, p3, base)
-    return last(blocks, p3, o3, base)
+    base = early(blocks, p1, o1, q2, across(after(q2, second_sent)))
+    q3 = after(exchange(second_sent), base)
+    q3_other = across(q3)
+    blocks, base = load(HEAD, STRIDE, 0, q3, base)
+    return last(blocks, q3, q3_other, base)
 
 
 def on_any(vectors, tile_blocks, block_rows, block_cols, counts):

time: 84 us -> 84.6 us (level)
  the two profiles are of different devices: /device:TPU:3 before, /device:TPU:0 now
where the time goes in v3:
time: 84.6 us; the launch traced here: 83.7 us
  blocking collectives  31.6 us (37%)
  Pallas kernels  27.6 us (33%)
  waiting for transfers between devices  12.5 us (15%)
  starting transfers between devices  8.26 us (10%)
  other arithmetic  1.61 us (2%)
  local copies, waits for them, and re-layouts  1.39 us (2%)
    pallas_call x9, Pallas kernels, call(): pl.pallas_call(kernel, out_shape=[space(shape, dtype) for shape, dtype, s...  27.6 us
    all_to_all x1, blocking collectives, on_pair(): q2 = exchange(first_sent)  18.5 us
    all_to_all x1, blocking collectives, on_pair(): wanted = exchange(jnp.broadcast_to(needed, (n_row, LANES)))  13.1 us
    all_to_all x1, waiting for transfers between devices, on_pair(): p1 = after(exchange(sent), plan, sent_other)  6.14 us
    all_to_all x1, waiting for transfers between devices, on_pair(): q3 = after(exchange(second_sent), base)  5.26 us
    all_to_all x1, starting transfers between devices, on_pair(): q3 = after(exchange(second_sent), base)  3.65 us
    all_to_all x1, starting transfers between devices, on_pair(): p1 = after(exchange(sent), plan, sent_other)  3.51 us
  transfers between devices with their start and end apart: 9, of which 4 were waited for; matrix products, arithmetic and copies ran while one was open for 2% of the time, Pallas kernels for 24%

profile of v3, /device:TPU:0, one launch (start us, length us, event | category | flops | bytes accessed | tf_op | source)
XLA Modules:
  0.0 83.7 jit_solution(16508662040995541566)
XLA Ops:
  0.0 0.5 collective-permute-start.3
  0.5 0.7 and_select_fusion.1
  1.1 0.1 select_reduce_fusion
  1.3 13.1 %all_to_all.23 = s32[8,1,128]{2,1,0:T(1,128)S(1)} all-to-all(s32[8,1,128]{2,1,0:T(1,128)S(1)} %broadcast_in_dim.21), channel_id=1, replica_groups=mesh['row'=8,'col'=2,'vec'=2] {'row'}, dimensions={0} | all-to-all | bytes 8192 | tf_op jit(solution)/shard_map/all_to_all | solution.py:421
  14.4 2.4 %pick.1.picked = bf16[8,256,128]{2,1,0:T(8,128)(2,1)} custom-call(s32[8,128]{1,0:T(8,128)S(1)} %bitcast.16, bf16[8192,128]{1,0:T(8,128)(2,1)} %vectors.3), custom_call_target="tpu_custom_call" | custom-call | tf_op jit(solution)/shard_map/pick/pallas_call | solution.py:377
  16.8 3.5 %all-to-all-start.1 = ((bf16[8,256,128]{2,1,0:T(8,128)(2,1)}), bf16[8,256,128]{2,1,0:T(8,128)(2,1)S(1)}, u32[]{:S(2)}, u32[]{:S(2)}) async-start(bf16[8,256,128]{2,1,0:T(8,128)(2,1)} %pick.1.picked), calls=%async_computation.1 | async-start | bytes 1048576 | tf_op jit(solution)/shard_map/all_to_all | solution.py:540
  21.1 0.8 pad_add_fusion.1
  21.8 0.5 collective-permute-start
  22.5 1.0 %collective-permute-done.1.meta_b = s32[65]{0:T(128)S(1)} collective-permute-done((s32[65]{0:T(128)S(1)}, s32[65]{0:T(128)S(1)}, u32[]{:S(2)}, u32[]{:S(2)}) %collective-permute-start.1) | collective-permute-done | bytes 292 | tf_op jit(solution)/shard_map/ppermute | solution.py:434
  23.4 0.7 copy-done
  24.1 0.7 copy-done.1
  24.8 3.4 %plan.1 = s32[1425]{0:T(1024)S(4)} custom-call(s32[2]{0:T(128)S(1)} %pad_add_fusion.place, s32[8,128]{1,0:T(8,128)S(1)} %bitcast.18, s32[8,128]{1,0:T(8,128)S(1)} %collective-permute-done.wanted_b, s32[32]{0:T(128)S(1)} %bitcast.22, s32[32]{0:T(128)S(1)} %bitcast.20, s32[1]{0:T(128)} %bitcast.15.used_a, s32[65]{0:T(128)S(1)} %collective-permute-done.1.meta_b), custom_call_target="tpu_custom_call" | custom-call | tf_op jit(solution)/shard_map/plan/pallas_call | solution.py:377
  28.2 6.1 %all-to-all-done.1.pieces = bf16[8,256,128]{2,1,0:T(8,128)(2,1)S(1)} async-done(((bf16[8,256,128]{2,1,0:T(8,128)(2,1)}), bf16[8,256,128]{2,1,0:T(8,128)(2,1)S(1)}, u32[]{:S(2)}, u32[]{:S(2)}) %all-to-all-start.1) | async-done | bytes 524320 | tf_op jit(solution)/shard_map/all_to_all | solution.py:540
  34.3 1.7 %load.3.blocks = bf16[64,256,256]{2,1,0:T(8,128)(2,1)S(1)} custom-call(s32[1425]{0:T(1024)S(4)} %plan.1, bf16[32,256,256]{2,1,0:T(8,128)(2,1)} %bitcast.24, bf16[32,256,256]{2,1,0:T(8,128)(2,1)} %collective-permute-done.3.tile_b), custom_call_target="tpu_custom_call" | custom-call | tf_op jit(solution)/shard_map/load/pallas_call | solution.py:377
  36.1 0.1 collective-permute-done.4.others
  36.2 1.7 %sent.2 = (bf16[8,256,128]{2,1,0:T(8,128)(2,1)S(1)}, bf16[8,256,128]{2,1,0:T(8,128)(2,1)S(1)}) custom-call(s32[1425]{0:T(1024)S(4)} %plan.1, bf16[64,256,256]{2,1,0:T(8,128)(2,1)S(1)} %load.3.blocks, bf16[8,256,128]{2,1,0:T(8,128)(2,1)S(1)} %all-to-all-done.1.pieces, bf16[8,256,128]{2,1,0:T(8,128)(2,1)S(1)} %collective-permute-done.4.others, ...), custom_call_target="tpu_custom_call" | custom-call | flops 134217728 | bytes 2621440 | tf_op jit(solution)/shard_map/sent/pallas_call | solution.py:377
  37.9 18.5 %all_to_all.24.pieces.mine = bf16[8,256,128]{2,1,0:T(8,128)(2,1)S(1)} all-to-all(bf16[8,256,128]{2,1,0:T(8,128)(2,1)S(1)} %get-tuple-element.21.current), channel_id=1, replica_groups=mesh['row'=8,'col'=2,'vec'=2] {'row'}, dimensions={0} | all-to-all | bytes 1048576 | tf_op jit(solution)/shard_map/all_to_all | solution.py:544
  56.4 1.9 %sent.3 = bf16[8,256,128]{2,1,0:T(8,128)(2,1)} custom-call(s32[1425]{0:T(1024)S(4)} %plan.1, bf16[64,256,256]{2,1,0:T(8,128)(2,1)S(1)} %load.3.blocks, bf16[8,256,128]{2,1,0:T(8,128)(2,1)S(1)} %all_to_all.24.pieces.mine, bf16[8,256,128]{2,1,0:T(8,128)(2,1)S(1)} %get-tuple-element.22.previous, bf16[8,256,128]{2,1,0:T(8,128)(2,1)S(1)} %get-tuple-element.21.current), custom_call_target="tpu_custom_call" | custom-call | flops 134217728 | bytes 2621440 | tf_op jit(solution)/shard_map/sent/pallas_call | solution.py:377
  58.3 3.6 %all-to-all-start.3 = ((bf16[8,256,128]{2,1,0:T(8,128)(2,1)}), bf16[8,256,128]{2,1,0:T(8,128)(2,1)S(1)}, u32[]{:S(2)}, u32[]{:S(2)}) async-start(bf16[8,256,128]{2,1,0:T(8,128)(2,1)} %sent.3), calls=%async_computation.3 | async-start | bytes 1048576 | tf_op jit(solution)/shard_map/all_to_all | solution.py:548
  62.0 2.5 %load.4.blocks = bf16[64,256,256]{2,1,0:T(8,128)(2,1)S(1)} custom-call(s32[1425]{0:T(1024)S(4)} %plan.1, bf16[32,256,256]{2,1,0:T(8,128)(2,1)} %bitcast.25, bf16[32,256,256]{2,1,0:T(8,128)(2,1)} %collective-permute-done.3.tile_b), custom_call_target="tpu_custom_call" | custom-call | tf_op jit(solution)/shard_map/load/pallas_call | solution.py:377
  64.5 6.8 %early.1.array = bf16[32,256,128]{2,1,0:T(8,128)(2,1)} custom-call(s32[1425]{0:T(1024)S(4)} %plan.1, bf16[64,256,256]{2,1,0:T(8,128)(2,1)S(1)} %load.4.blocks, bf16[8,256,128]{2,1,0:T(8,128)(2,1)S(1)} %all-to-all-done.1.pieces, bf16[8,256,128]{2,1,0:T(8,128)(2,1)S(1)} %collective-permute-done.4.others, bf16[8,256,128]{2,1,0:T(8,128)(2,1)S(1)} %all_to_all.24.pieces.mine, ...), custom_call_target="tpu_custom_call" | custom-call | flops 1073741824 | bytes 20971520 | tf_op jit(solution)/shard_map/early/pallas_call | solution.py:377
  71.4 5.3 %all-to-all-done.3.mine = bf16[8,256,128]{2,1,0:T(8,128)(2,1)S(1)} async-done(((bf16[8,256,128]{2,1,0:T(8,128)(2,1)}), bf16[8,256,128]{2,1,0:T(8,128)(2,1)S(1)}, u32[]{:S(2)}, u32[]{:S(2)}) %all-to-all-start.3) | async-done | bytes 524320 | tf_op jit(solution)/shard_map/all_to_all | solution.py:548
  76.6 3.0 %load.5 = (bf16[64,256,256]{2,1,0:T(8,128)(2,1)S(1)}, bf16[32,256,128]{2,1,0:T(8,128)(2,1)S(1)}) custom-call(s32[1425]{0:T(1024)S(4)} %plan.1, bf16[32,256,256]{2,1,0:T(8,128)(2,1)} %bitcast.26, bf16[32,256,256]{2,1,0:T(8,128)(2,1)} %collective-permute-done.3.tile_b, bf16[32,256,128]{2,1,0:T(8,128)(2,1)} %early.1.array), custom_call_target="tpu_custom_call" | custom-call | tf_op jit(solution)/shard_map/load/pallas_call | solution.py:377
  79.7 4.0 %last.1 = bf16[32,256,128]{2,1,0:T(8,128)(2,1)} custom-call(s32[1425]{0:T(1024)S(4)} %plan.1, bf16[64,256,256]{2,1,0:T(8,128)(2,1)S(1)} %get-tuple-element.27.blocks, bf16[8,256,128]{2,1,0:T(8,128)(2,1)S(1)} %all-to-all-done.3.mine, bf16[8,256,128]{2,1,0:T(8,128)(2,1)S(1)} %collective-permute-done.6.other, bf16[32,256,128]{2,1,0:T(8,128)(2,1)S(1)} %get-tuple-element.28.base), custom_call_target="tpu_custom_call" | custom-call | flops 536870912 | bytes 10485760 | tf_op jit(solution)/shard_map/last/pallas_call | solution.py:377
  (16 shorter events, 0.3 us)
Async XLA Ops:
  0.0 34.3 %collective-permute-start.3 = (bf16[32,256,256]{2,1,0:T(8,128)(2,1)}, bf16[32,256,256]{2,1,0:T(8,128)(2,1)}, u32[]{:S(2)}, u32[]{:S(2)}) collective-permute-start(bf16[32,256,256]{2,1,0:T(8,128)(2,1)} %bitcast.23), channel_id=1, source_target_pairs={{0,2},{2,0},{1,3},{3,1},{4,6},{6,4},{5,7},{7,5},{8,10},{10,8},{9,1... | collective-permute-start | bytes 12582920 | tf_op jit(solution)/shard_map/ppermute | solution.py:432
  16.8 17.5 %all-to-all-start.1 = ((bf16[8,256,128]{2,1,0:T(8,128)(2,1)}), bf16[8,256,128]{2,1,0:T(8,128)(2,1)S(1)}, u32[]{:S(2)}, u32[]{:S(2)}) async-start(bf16[8,256,128]{2,1,0:T(8,128)(2,1)} %pick.1.picked), calls=%async_computation.1 | async-start | bytes 1048576 | tf_op jit(solution)/shard_map/all_to_all | solution.py:540
  20.3 7.8 %collective-permute-start.2 = (bf16[8,256,128]{2,1,0:T(8,128)(2,1)}, bf16[8,256,128]{2,1,0:T(8,128)(2,1)S(1)}, u32[]{:S(2)}, u32[]{:S(2)}) collective-permute-start(bf16[8,256,128]{2,1,0:T(8,128)(2,1)} %pick.1.picked), channel_id=1, source_target_pairs={{0,2},{2,0},{1,3},{3,1},{4,6},{6,4},{5,7},{7,5},{8,10},{10,8},{9,1... | collective-permute-start | bytes 1572872 | tf_op jit(solution)/shard_map/ppermute | solution.py:435
  21.8 1.6 %collective-permute-start = (s32[8,128]{1,0:T(8,128)S(1)}, s32[8,128]{1,0:T(8,128)S(1)}, u32[]{:S(2)}, u32[]{:S(2)}) collective-permute-start(s32[8,128]{1,0:T(8,128)S(1)} %bitcast.17), channel_id=1, source_target_pairs={{0,2},{2,0},{1,3},{3,1},{4,6},{6,4},{5,7},{7,5},{8,10},{10,8},{9,1... | collective-permute-start | bytes 12296 | tf_op jit(solution)/shard_map/ppermute | solution.py:433
  22.3 1.1 %collective-permute-start.1 = (s32[65]{0:T(128)S(1)}, s32[65]{0:T(128)S(1)}, u32[]{:S(2)}, u32[]{:S(2)}) collective-permute-start(s32[65]{0:T(128)S(1)} %pad_add_fusion.1), channel_id=1, source_target_pairs={{0,2},{2,0},{1,3},{3,1},{4,6},{6,4},{5,7},{7,5},{8,10},{10,8},{9,1... | collective-permute-start | bytes 788 | tf_op jit(solution)/shard_map/ppermute | solution.py:434
  23.4 0.7 copy-start
  24.1 0.7 copy-start.1
  28.2 7.9 %copy-start.2 = (bf16[8,256,128]{2,1,0:T(8,128)(2,1)}, bf16[8,256,128]{2,1,0:T(8,128)(2,1)S(1)}, u32[]{:S(2)}) copy-start(bf16[8,256,128]{2,1,0:T(8,128)(2,1)S(1)} %collective-permute-done.2.picked_b) | copy-start | bytes 1572868
  34.3 1.9 %collective-permute-start.4 = (bf16[8,256,128]{2,1,0:T(8,128)(2,1)S(1)}, bf16[8,256,128]{2,1,0:T(8,128)(2,1)S(1)}, u32[]{:S(2)}, u32[]{:S(2)}) collective-permute-start(bf16[8,256,128]{2,1,0:T(8,128)(2,1)S(1)} %all-to-all-done.1.pieces), channel_id=1, source_target_pairs={{0,2},{2,0},{1,3},{3,1},{4,6},{6,4},{5,7},{7,5},{8,10},{10,8},{9,1... | collective-permute-start | bytes 1572872 | tf_op jit(solution)/shard_map/ppermute | solution.py:541
  58.3 18.3 %all-to-all-start.3 = ((bf16[8,256,128]{2,1,0:T(8,128)(2,1)}), bf16[8,256,128]{2,1,0:T(8,128)(2,1)S(1)}, u32[]{:S(2)}, u32[]{:S(2)}) async-start(bf16[8,256,128]{2,1,0:T(8,128)(2,1)} %sent.3), calls=%async_computation.3 | async-start | bytes 1048576 | tf_op jit(solution)/shard_map/all_to_all | solution.py:548
  62.0 2.5 %collective-permute-start.5 = (bf16[8,256,128]{2,1,0:T(8,128)(2,1)S(1)}, bf16[8,256,128]{2,1,0:T(8,128)(2,1)S(1)}, u32[]{:S(2)}, u32[]{:S(2)}) collective-permute-start(bf16[8,256,128]{2,1,0:T(8,128)(2,1)S(1)} %all_to_all.24.pieces.mine), channel_id=1, source_target_pairs={{0,2},{2,0},{1,3},{3,1},{4,6},{6,4},{5,7},{7,5},{8,10},{10,8},{9,1... | collective-permute-start | bytes 1572872 | tf_op jit(solution)/shard_map/ppermute | solution.py:547
  76.6 3.0 %collective-permute-start.6 = (bf16[8,256,128]{2,1,0:T(8,128)(2,1)S(1)}, bf16[8,256,128]{2,1,0:T(8,128)(2,1)S(1)}, u32[]{:S(2)}, u32[]{:S(2)}) collective-permute-start(bf16[8,256,128]{2,1,0:T(8,128)(2,1)S(1)} %all-to-all-done.3.mine), channel_id=1, source_target_pairs={{0,2},{2,0},{1,3},{3,1},{4,6},{6,4},{5,7},{7,5},{8,10},{10,8},{9,1... | collective-permute-start | bytes 1572872 | tf_op jit(solution)/shard_map/ppermute | solution.py:549
